TPU v7x, 256 devices: a whole 4x4x8 slice. The times are simulated.
256 devices in a mesh: tx: 8 (over z), ty: 16 (over x, y), scan: 2 (over core).
Axes of the slice: x: 4, y: 4, z: 8, core: 2. Of those that a mesh axis runs over, the one named last changes fastest.
Arguments:
- object_slices: float32 [2, 2, 4096, 8192], P(None, None, 'tx', 'ty'), may hold values from -3 to 3
- probe_modes: float32 [2, 2, 256, 256], replicated, may hold values from -5 to 5
- offsets: int32 [256, 2], P(('tx', 'ty', 'scan')), may hold values from 0 to 511, as said below
- measured: float32 [256, 256, 256], P(('tx', 'ty', 'scan')), may hold values from 0.25 to 8
Outputs:
- object_grad: float32 [2, 2, 4096, 8192], P(None, None, 'tx', 'ty')
- probe_grad: float32 [2, 2, 256, 256], replicated
Inputs may be any that keep to these rules, and one draw needn't show every extreme that they name: `offsets`: the position is held by the device of its tile; every patch lies inside the object, so in the last tile row the row offset is at most 256 and in the last tile column the column offset is at most 256.
All inputs are finite; a program needn't handle non-finite values.
Results may differ from a plain program's by a relative error of at most 0.0003.
Values sent between devices are 32-bit elements; how exact they have to be, the bound alone decides.
No kernel may reach another device: no remote copies, remote signals or barrier semaphores. Data moves between devices by JAX's collectives and lax.ppermute only.
A program may use at most 128 MiB of HBM per device.

v0:
```python
import math

import jax
import jax.numpy as jnp
from jax import lax
from jax.sharding import PartitionSpec as P

fresnel_number = 6.0


def from_behind(block, axis, distance):
    devices = range(lax.axis_size(axis))
    route = [(i - distance, i) for i in devices if i - distance in devices]
    return lax.ppermute(block, axis, route)


def dft_tables(extent):
    counter = lax.iota(jnp.int32, extent)
    product = counter[:, None] * counter[None, :] % extent
    angle = 2.0 * jnp.pi / extent * product.astype(jnp.float32)
    norm_factor = 1.0 / math.sqrt(extent)
    return (jnp.cos(angle) * norm_factor, -jnp.sin(angle) * norm_factor)


def chirp_kernel(extent):
    counter = lax.iota(jnp.int32, extent)
    freqs = (counter + extent // 2) % extent - extent // 2
    squares = (freqs * freqs).astype(jnp.float32)
    phase = jnp.pi * fresnel_number * (squares[:, None] + squares[None, :]) / float(extent * extent)
    return (jnp.cos(phase), -jnp.sin(phase))


def left_product(table, field):
    return jnp.einsum("ab,mbc->mac", table, field, precision=lax.Precision.HIGHEST)


def right_product(field, table):
    return jnp.einsum("mab,bc->mac", field, table, precision=lax.Precision.HIGHEST)


def transform(real_part, imag_part, cos_table, sin_table):
    left_real = left_product(cos_table, real_part) - left_product(sin_table, imag_part)
    left_imag = left_product(cos_table, imag_part) + left_product(sin_table, real_part)
    out_real = right_product(left_real, cos_table) - right_product(left_imag, sin_table)
    out_imag = right_product(left_real, sin_table) + right_product(left_imag, cos_table)
    return (out_real, out_imag)


def position_error(cells, modes, target, tables):
    cos_table, sin_table, kernel_real, kernel_imag = tables
    layer_real = cells[:, 0]
    layer_imag = cells[:, 1]
    wave_real = modes[:, 0] * layer_real[0] - modes[:, 1] * layer_imag[0]
    wave_imag = modes[:, 0] * layer_imag[0] + modes[:, 1] * layer_real[0]
    spec_real, spec_imag = transform(wave_real, wave_imag, cos_table, sin_table)
    mixed_real = kernel_real * spec_real - kernel_imag * spec_imag
    mixed_imag = kernel_real * spec_imag + kernel_imag * spec_real
    back_real, back_imag = transform(mixed_real, mixed_imag, cos_table, -sin_table)
    wave_real = back_real * layer_real[1] - back_imag * layer_imag[1]
    wave_imag = back_real * layer_imag[1] + back_imag * layer_real[1]
    far_real, far_imag = transform(wave_real, wave_imag, cos_table, sin_table)
    intensity = jnp.sum(far_real * far_real + far_imag * far_imag, axis=0)
    return 0.5 * jnp.sum((intensity - target) ** 2)


def return_spill(grad_field, tile_rows, tile_cols, width):
    spill_cols = from_behind(grad_field[:, :, :, tile_cols:], "ty", 1)
    narrow = grad_field[:, :, :, :tile_cols]
    narrow = narrow.at[:, :, :, :width].add(spill_cols)
    spill_rows = from_behind(narrow[:, :, tile_rows:, :], "tx", 1)
    tile_grad = narrow[:, :, :tile_rows, :]
    return tile_grad.at[:, :, :width, :].add(spill_rows)


def body(object_slices, probe_modes, offsets, measured):
    width = probe_modes.shape[-1]
    layer_count = object_slices.shape[0]
    tile_rows = object_slices.shape[2]
    tile_cols = object_slices.shape[3]
    below = from_behind(object_slices[:, :, :width, :], "tx", -1)
    taller = jnp.concatenate([object_slices, below], axis=2)
    beside = from_behind(taller[:, :, :, :width], "ty", -1)
    extended = jnp.concatenate([taller, beside], axis=3)
    cos_table, sin_table = dft_tables(width)
    kernel_real, kernel_imag = chirp_kernel(width)
    tables = (cos_table, sin_table, kernel_real, kernel_imag)

    def visit(carry, inputs):
        grad_field, grad_modes = carry
        shift_pair, target = inputs
        zero = jnp.int32(0)
        starts = (zero, zero, shift_pair[0], shift_pair[1])
        cells = lax.dynamic_slice(extended, starts, (layer_count, 2, width, width))
        value, pullback = jax.vjp(
            lambda cells_in, modes_in: position_error(cells_in, modes_in, target, tables),
            cells,
            probe_modes,
        )
        grad_cells, grad_probe = pullback(jnp.ones_like(value))
        current = lax.dynamic_slice(grad_field, starts, (layer_count, 2, width, width))
        grad_field = lax.dynamic_update_slice(grad_field, current + grad_cells, starts)
        return ((grad_field, grad_modes + grad_probe), None)

    start_state = (jnp.zeros_like(extended), jnp.zeros_like(probe_modes))
    (grad_field, grad_modes), _ = lax.scan(visit, start_state, (offsets, measured))
    tile_grad = return_spill(grad_field, tile_rows, tile_cols, width)
    tile_grad = lax.psum(tile_grad, "scan")
    total_modes = lax.psum(grad_modes, ("tx", "ty", "scan"))
    position_total = (
        lax.axis_size("tx") * lax.axis_size("ty") * lax.axis_size("scan") * offsets.shape[0]
    )
    return (tile_grad, total_modes / position_total)


def solution(mesh):
    placed = (
        P(None, None, "tx", "ty"),
        P(),
        P(("tx", "ty", "scan"), None),
        P(("tx", "ty", "scan"), None, None),
    )
    return jax.shard_map(
        body,
        mesh=mesh,
        in_specs=placed,
        out_specs=(P(None, None, "tx", "ty"), P()),
        check_vma=False,
    )
```

profile of v0, /device:TPU:57, one launch (start us, length us, event | category | flops | bytes accessed | tf_op | source)
XLA Modules:
  0.0 645.7 jit_solution(12042363486230819528)
XLA Ops:
  11.5 46.4 %collective-permute-done = f32[2,2,256,512]{3,2,1,0:T(8,128)S(1)} collective-permute-done((f32[2,2,256,512]{3,2,1,0:T(8,128)S(1)}, f32[2,2,256,512]{3,2,1,0:T(8,128)S(1)}, u32[]{:S(2)}, u32[]{:S(2)}) %collective-permute-start) | collective-permute-done | bytes 2097184 | tf_op jit(solution)/shard_map/ppermute | solution.py:14
  58.1 2.7 copy-done.1
  60.8 2.0 slice.146
  62.8 2.4 collective-permute-start.1
  71.1 64.2 %collective-permute-done.1 = f32[2,2,768,256]{3,2,1,0:T(8,128)} collective-permute-done((f32[2,2,768,256]{3,2,1,0:T(8,128)}, f32[2,2,768,256]{3,2,1,0:T(8,128)}, u32[]{:S(2)}, u32[]{:S(2)}) %collective-permute-start.1) | collective-permute-done | bytes 3145760 | tf_op jit(solution)/shard_map/ppermute | solution.py:14
  135.4 2.1 fusion.20
  157.5 2.0 fusion.44
  168.8 2.1 fusion.92
  193.8 2.8 multiply_reduce_fusion.3
  222.1 4.2 multiply_bitcast_fusion.3
  231.9 4.4 broadcast_in_dim.60
  236.4 12.1 %dynamic_update_slice.4 = f32[2,2,768,768]{3,2,1,0:T(8,128)} dynamic-update-slice(f32[2,2,768,768]{3,2,1,0:T(8,128)} %broadcast_in_dim.60, f32[2,2,256,256]{3,2,1,0:T(8,128)S(1)} %copy.145, s32[]{:T(128)} %constant.106.clone.1, s32[]{:T(128)} %constant.106.clone.1, s32[]{:T(128)S(6)} %select_n.142, s32[]{:T(128)S(6)} %select_n.143) | dynamic-update-slice | bytes 2097156 | tf_op jit(solution)/shard_map/while/body/eval_jaxpr/dynamic_update_slice | solution.py:101
  248.5 2.1 slice.153
  252.5 3.5 slice.151
  256.0 64.0 %collective-permute-done.2 = f32[2,2,768,256]{3,2,1,0:T(8,128)S(1)} collective-permute-done((f32[2,2,768,256]{3,2,1,0:T(8,128)S(1)}, f32[2,2,768,256]{3,2,1,0:T(8,128)S(1)}, u32[]{:S(2)}, u32[]{:S(2)}) %collective-permute-start.2) | collective-permute-done | bytes 3145760 | tf_op jit(solution)/shard_map/ppermute | solution.py:14
  320.0 2.5 fusion
  322.6 2.7 copy-done
  326.7 3.7 collective-permute-start.3
  331.6 4.6 slice.154
  336.3 38.4 %collective-permute-done.3 = f32[2,2,256,512]{3,2,1,0:T(8,128)S(1)} collective-permute-done((f32[2,2,256,512]{3,2,1,0:T(8,128)}, f32[2,2,256,512]{3,2,1,0:T(8,128)S(1)}, u32[]{:S(2)}, u32[]{:S(2)}) %collective-permute-start.3) | collective-permute-done | bytes 2097184 | tf_op jit(solution)/shard_map/ppermute | solution.py:14
  374.7 3.4 fusion.1
  378.2 212.2 %all-reduce.19.cloned.1.call-done = f32[2,2,256,256]{2,3,0,1:T(8,128)} async-done(((f32[2,2,256,256]{2,3,0,1:T(8,128)}), f32[2,2,256,256]{2,3,0,1:T(8,128)}) %all-reduce.19.cloned.1.call-update) | async-done | bytes 1048592 | tf_op jit(solution)/shard_map/psum | solution.py:108
  592.9 40.9 %all-reduce.17.cloned.1.call-done = f32[2,2,512,512]{3,2,1,0:T(8,128)} async-done(((f32[2,2,512,512]{3,2,1,0:T(8,128)}), f32[2,2,512,512]{3,2,1,0:T(8,128)}) %all-reduce.17.cloned.1.call-update) | async-done | bytes 4194320 | tf_op jit(solution)/shard_map/psum | solution.py:107
  633.8 4.6 copy.195
  (94 shorter events, 96.7 us)
Async XLA Ops:
  7.2 583.1 %all-reduce.19.cloned.1.call-start = ((), (), s32[]{:S(2)}) async-start(), calls=%async_computation.1 | async-start | bytes 2097152 | tf_op jit(solution)/shard_map/psum | solution.py:108
  7.2 3.9 copy-start.2
  9.1 48.8 %collective-permute-start = (f32[2,2,256,512]{3,2,1,0:T(8,128)S(1)}, f32[2,2,256,512]{3,2,1,0:T(8,128)S(1)}, u32[]{:S(2)}, u32[]{:S(2)}) collective-permute-start(f32[2,2,256,512]{3,2,1,0:T(8,128)S(1)} %slice.131), channel_id=1, source_target_pairs={{32,0},{64,32},{96,64},{128,96},{160,128},{192,160},{224,192},{33,... | collective-permute-start | bytes 6291464 | tf_op jit(solution)/shard_map/ppermute | solution.py:14
  11.5 53.6 %copy-start.10 = (s32[1,2]{1,0:T(1,128)S(1)}, s32[1,2]{1,0:T(1,128)}, u32[]{:S(2)}) copy-start(s32[1,2]{1,0:T(1,128)} %param.10) | copy-start | bytes 28
  58.1 2.7 copy-start.1
  60.8 7.6 %copy-start.8 = (f32[2,2,256,256]{3,2,1,0:T(8,128)S(1)}, f32[2,2,256,256]{3,2,1,0:T(8,128)}, u32[]{:S(2)}) copy-start(f32[2,2,256,256]{3,2,1,0:T(8,128)} %param.9) | copy-start | bytes 3145732
  62.8 72.6 %collective-permute-start.1 = (f32[2,2,768,256]{3,2,1,0:T(8,128)}, f32[2,2,768,256]{3,2,1,0:T(8,128)}, u32[]{:S(2)}, u32[]{:S(2)}) collective-permute-start(f32[2,2,768,256]{3,2,1,0:T(8,128)} %slice.146), channel_id=1, source_target_pairs={{2,0},{4,2},{6,4},{8,6},{10,8},{12,10},{14,12},{16,14},{18,16},{20... | collective-permute-start | bytes 9437192 | tf_op jit(solution)/shard_map/ppermute | solution.py:14
  174.6 7.4 %copy-start.9 = (f32[1,256,256]{2,1,0:T(8,128)S(1)}, f32[1,256,256]{2,1,0:T(8,128)}, u32[]{:S(2)}) copy-start(f32[1,256,256]{2,1,0:T(8,128)} %param.11) | copy-start | bytes 786436
  222.0 8.6 %copy-start.6 = (f32[256,256]{1,0:T(8,128)S(1)}, f32[256,256]{1,0:T(8,128)}, u32[]{:S(2)}) copy-start(f32[256,256]{1,0:T(8,128)} %get-tuple-element.66) | copy-start | bytes 786436
  222.1 8.6 %copy-start.7 = (f32[256,256]{1,0:T(8,128)S(1)}, f32[256,256]{1,0:T(8,128)}, u32[]{:S(2)}) copy-start(f32[256,256]{1,0:T(8,128)} %get-tuple-element.67) | copy-start | bytes 786436
  250.6 69.4 %collective-permute-start.2 = (f32[2,2,768,256]{3,2,1,0:T(8,128)S(1)}, f32[2,2,768,256]{3,2,1,0:T(8,128)S(1)}, u32[]{:S(2)}, u32[]{:S(2)}) collective-permute-start(f32[2,2,768,256]{3,2,1,0:T(8,128)S(1)} %slice.153), channel_id=1, source_target_pairs={{0,2},{2,4},{4,6},{6,8},{8,10},{10,12},{12,14},{14,16},{16,18},{18... | collective-permute-start | bytes 9437192 | tf_op jit(solution)/shard_map/ppermute | solution.py:14
  322.5 2.7 copy-start
  325.2 5.2 copy-start.3
  325.2 5.2 copy-start.4
  325.2 5.2 copy-start.5
  326.7 48.0 %collective-permute-start.3 = (f32[2,2,256,512]{3,2,1,0:T(8,128)}, f32[2,2,256,512]{3,2,1,0:T(8,128)S(1)}, u32[]{:S(2)}, u32[]{:S(2)}) collective-permute-start(f32[2,2,256,512]{3,2,1,0:T(8,128)} %slice.156), channel_id=1, source_target_pairs={{0,32},{32,64},{64,96},{96,128},{128,160},{160,192},{192,224},{1,3... | collective-permute-start | bytes 6291464 | tf_op jit(solution)/shard_map/ppermute | solution.py:14
  331.6 302.2 %all-reduce.17.cloned.1.call-start = ((), (), s32[]{:S(2)}) async-start(), calls=%async_computation | async-start | bytes 8388608 | tf_op jit(solution)/shard_map/psum | solution.py:107
Sparse Core Ops, SparseCore 0:
  331.7 258.5 all-reduce.18
  593.8 39.9 all-reduce.16
where the time goes:
time: 658 us; the launch traced here: 646 us
  waiting for transfers between devices  466 us (71%)
  matrix products  88.1 us (13%)
  local copies, waits for them, and re-layouts  50 us (8%)
  between operations  19 us (3%)
  other arithmetic  12.6 us (2%)
  starting transfers between devices  9.98 us (2%)
    ppermute x4, waiting for transfers between devices, from_behind(): return lax.ppermute(block, axis, route)  213 us
    psum x1, waiting for transfers between devices, body(): total_modes = lax.psum(grad_modes, ('tx', 'ty', 'scan'))  212 us
    dot_general x24, matrix products, left_product(): jnp.einsum('ab,mbc->mac', table, field, precision=lax.Precision.HIGHEST)  46.2 us
    dot_general x24, matrix products, right_product(): jnp.einsum('mab,bc->mac', field, table, precision=lax.Precision.HIGHEST)  41.8 us
    psum x1, waiting for transfers between devices, body(): tile_grad = lax.psum(tile_grad, 'scan')  40.9 us
  transfers between devices with their start and end apart: 6, of which 6 were waited for; matrix products, arithmetic and copies ran while one was open for 3% of the time, Pallas kernels for 0%

commit v1 on v0

v1 whole, which is shorter than its diff:
```python
import functools
import math

import jax
import jax.numpy as jnp
import ml_dtypes
import numpy as np
from jax import lax
from jax.experimental import pallas as pl
from jax.experimental.pallas import tpu as pltpu
from jax.sharding import PartitionSpec as P

fresnel_number = 6.0
W = 256
B16 = jnp.bfloat16
F32 = jnp.float32


def real_form(matrix):
    return np.block([[matrix.real, -matrix.imag], [matrix.imag, matrix.real]])


def tables():
    half = W // 2
    n = np.arange(half)
    norm = 1.0 / math.sqrt(W)
    even = np.exp(-2j * np.pi * np.outer(2 * n, n) / W) * norm
    odd = np.exp(-2j * np.pi * np.outer(2 * n + 1, n) / W) * norm
    k = np.arange(W)
    q = (k + half) % W - half
    h = np.exp(-1j * np.pi * fresnel_number * q.astype(np.float64) ** 2 / float(W * W))
    taps = np.fft.ifft(h)
    diff = (n[:, None] - n[None, :]) % W
    near, far = taps[diff], taps[(diff + half) % W]
    mats = [even, odd, 0.5 * (near + far), 0.5 * (near - far)]
    forms = []
    for m in mats:
        r = real_form(m)
        forms += [r, r.T]
    full = np.stack(forms)
    hi = full.astype(ml_dtypes.bfloat16)
    lo = (full - hi.astype(np.float64)).astype(ml_dtypes.bfloat16)
    return np.stack([hi, lo], axis=1)


E_L, E_T, O_L, O_T, U_L, U_T, V_L, V_T = range(8)


def deinterleave():
    order = np.concatenate([np.arange(0, W, 2), np.arange(1, W, 2)])
    p = np.zeros((W, W), np.float32)
    p[np.arange(W), order] = 1.0
    return np.stack([p, p.T]).astype(ml_dtypes.bfloat16)


def dot(a, b):
    return jnp.dot(a, b, preferred_element_type=F32)


def split(x):
    hi = x.astype(B16)
    return hi, (x - hi.astype(F32)).astype(B16)


def times(tab, which, x, axis):
    hi, lo = split(x)
    t_hi, t_lo = tab[which, 0], tab[which, 1]
    if axis == 0:
        return dot(t_hi, hi) + (dot(t_hi, lo) + dot(t_lo, hi))
    return dot(hi, t_hi) + (dot(lo, t_hi) + dot(hi, t_lo))


def halves(x, axis):
    h = W // 2
    return (x[:h], x[h:]) if axis == 0 else (x[:, :h], x[:, h:])


def butterfly(re, im, axis):
    r0, r1 = halves(re, axis)
    i0, i1 = halves(im, axis)
    u = jnp.concatenate([r0 + r1, i0 + i1], axis)
    v = jnp.concatenate([r0 - r1, i0 - i1], axis)
    return u, v


def join(a, b, axis):
    ar, ai = halves(a, axis)
    br, bi = halves(b, axis)
    return jnp.concatenate([ar, br], axis), jnp.concatenate([ai, bi], axis)


def one_axis(tab, kind, re, im, axis):
    left = axis == 0
    if kind == "inv":
        r0, r1 = halves(re, axis)
        i0, i1 = halves(im, axis)
        u, v = jnp.concatenate([r0, i0], axis), jnp.concatenate([r1, i1], axis)
    else:
        u, v = butterfly(re, im, axis)
    pick = {
        "fwd": (E_L, O_L) if left else (E_T, O_T),
        "inv": (E_T, O_T) if left else (E_L, O_L),
        "prop": (U_L, V_L) if left else (U_T, V_T),
        "back": (U_T, V_T) if left else (U_L, V_L),
    }[kind]
    a = times(tab, pick[0], u, axis)
    b = times(tab, pick[1], v, axis)
    if kind != "fwd":
        a, b = a + b, a - b
    return join(a, b, axis)


def both_axes(tab, kind, re, im):
    re, im = one_axis(tab, kind, re, im, 0)
    return one_axis(tab, kind, re, im, 1)


def cmul(ar, ai, br, bi):
    return ar * br - ai * bi, ar * bi + ai * br


def cmul_conj(ar, ai, br, bi):
    return ar * br + ai * bi, ar * bi - ai * br


def iotas():
    return (
        lax.broadcasted_iota(jnp.int32, (W, W), 0),
        lax.broadcasted_iota(jnp.int32, (W, W), 1),
    )


def block(q):
    return pl.ds(pl.multiple_of(q * W, W), W)


def prep_kernel(off, obj, probe, meas, perm, own_out, probe_out, meas_out):
    qr, tr = off[0] // W, off[0] % W
    qc, tc = off[1] // W, off[1] % W
    rho, gam = iotas()
    low_r, low_c = rho < tr, gam < tc
    for layer in range(2):
        for p in range(2):
            a = jnp.where(low_c, obj[layer, p, block(qr), W:], obj[layer, p, block(qr), block(qc)])
            b = jnp.where(low_c, obj[layer, p, W:, W:], obj[layer, p, W:, block(qc)])
            own_out[layer, p] = jnp.where(low_r, b, a)
    for m in range(2):
        for p in range(2):
            x = pltpu.roll(probe[m, p], tr, 0)
            probe_out[m, p] = pltpu.roll(x, tc, 1)

    def exact(x):
        hi, rest = x.astype(B16), None
        rest = x - hi.astype(F32)
        mid = rest.astype(B16)
        low = (rest - mid.astype(F32)).astype(B16)
        return hi, mid, low

    hi, mid, low = exact(meas[...])
    x = dot(perm[0], hi) + dot(perm[0], mid) + dot(perm[0], low)
    hi, mid, low = exact(x)
    meas_out[...] = dot(hi, perm[1]) + dot(mid, perm[1]) + dot(low, perm[1])


def whole_patch(off, own, below, right, diag):
    qr, tr = off[0] // W, off[0] % W
    qc, tc = off[1] // W, off[1] % W
    rho, gam = iotas()
    low_r, low_c = rho < tr, gam < tc
    halo_r = rho < tr * qr
    halo_c = gam < tc * qc
    below_v = jnp.where(low_c, below[:, W:], below[:, block(qc)])
    right_v = jnp.where(low_r, right[W:, :], right[block(qr), :])
    out = jnp.where(halo_r, below_v, own)
    return jnp.where(halo_c, jnp.where(halo_r, diag[...], right_v), out)


def patch_planes(scal, own, halo_mine, halo_other, out):
    s = scal[2]
    out[s] = whole_patch(scal, own[s], *halo_mine)
    out[1 - s] = whole_patch(scal, own[1 - s], *halo_other)


def first_kernel(scal, own, b0, r0, d0, b1, r1, d1, probe, tab, obj_out, back_out):
    patch_planes(scal, own, (b0, r0, d0), (b1, r1, d1), obj_out)
    o_r, o_i = obj_out[0], obj_out[1]
    for m in range(2):
        re, im = cmul(probe[m, 0], probe[m, 1], o_r, o_i)
        re, im = both_axes(tab, "prop", re, im)
        back_out[m, 0] = re
        back_out[m, 1] = im


def middle_kernel(scal, own, b0, r0, d0, b1, r1, d1, back, meas, tab, grad_out, wave_out, obj, far):
    patch_planes(scal, own, (b0, r0, d0), (b1, r1, d1), obj)
    for m in range(2):
        re, im = cmul(back[m, 0], back[m, 1], obj[0], obj[1])
        re, im = both_axes(tab, "fwd", re, im)
        far[m, 0] = re
        far[m, 1] = im
    inten = far[0, 0] ** 2 + far[0, 1] ** 2 + far[1, 0] ** 2 + far[1, 1] ** 2
    resid = 2.0 * (inten - meas[...])
    g_r = g_i = None
    for m in range(2):
        re, im = both_axes(tab, "inv", resid * far[m, 0], resid * far[m, 1])
        a, b = cmul_conj(back[m, 0], back[m, 1], re, im)
        g_r, g_i = (a, b) if g_r is None else (g_r + a, g_i + b)
        wave_out[m, 0], wave_out[m, 1] = cmul_conj(obj[0], obj[1], re, im)
    grad_out[0] = g_r
    grad_out[1] = g_i


def last_kernel(scal, wave, obj, probe, tab, grad_out, probe_out):
    tr, tc = scal[0] % W, scal[1] % W
    g_r = g_i = None
    for m in range(2):
        re, im = both_axes(tab, "back", wave[m, 0], wave[m, 1])
        a, b = cmul_conj(probe[m, 0], probe[m, 1], re, im)
        g_r, g_i = (a, b) if g_r is None else (g_r + a, g_i + b)
        for p, x in enumerate(cmul_conj(obj[0], obj[1], re, im)):
            x = pltpu.roll(x * (1.0 / 256.0), (W - tr) % W, 0)
            probe_out[m, p] = pltpu.roll(x, (W - tc) % W, 1)
    grad_out[0] = g_r
    grad_out[1] = g_i


def spread_kernel(scal, mine, other, own_out, below_out, right_out, diag_out):
    rho, gam = iotas()

    def band(index, q, t, i):
        return ((index >= t) & (q == i)) | ((index < t) & (q + 1 == i))

    where = []
    for k in range(2):
        r, c = scal[2 * k], scal[2 * k + 1]
        rows = [band(rho, r // W, r % W, i) for i in range(3)]
        cols = [band(gam, c // W, c % W, j) for j in range(3)]
        where.append((rows, cols))
    a, b = mine[...], other[...]
    for i in range(3):
        for j in range(3):
            v = jnp.where(where[0][0][i] & where[0][1][j], a, 0.0) + jnp.where(
                where[1][0][i] & where[1][1][j], b, 0.0
            )
            if i < 2 and j < 2:
                own_out[i * W : (i + 1) * W, j * W : (j + 1) * W] = v
            elif i < 2:
                right_out[i * W : (i + 1) * W, :] = v
            elif j < 2:
                below_out[:, j * W : (j + 1) * W] = v
            else:
                diag_out[...] = v


def finish_kernel(scal, own0, b0, r0, d0, own1, b1, r1, d1, out):
    s = scal[0]
    for plane, own, b, r, d in ((s, own0, b0, r0, d0), (1 - s, own1, b1, r1, d1)):
        out[plane, W:, W:] = own[W:, W:]
        out[plane, :W, :W] = own[:W, :W] + (b[:, :W] + r[:W, :] + d[...])
        out[plane, :W, W:] = own[:W, W:] + b[:, W:]
        out[plane, W:, :W] = own[W:, :W] + r[W:, :]


def call(kernel, outs, args, flops=0, scratch=()):
    spec = pl.BlockSpec(memory_space=pltpu.VMEM)
    moved = 4 * sum(math.prod(o) for o in outs) + sum(a.size * a.dtype.itemsize for a in args)
    return pl.pallas_call(
        kernel,
        out_shape=[jax.ShapeDtypeStruct(o, F32) for o in outs],
        in_specs=[pl.BlockSpec(memory_space=pltpu.SMEM)] + [spec] * (len(args) - 1),
        out_specs=[spec] * len(outs),
        scratch_shapes=[pltpu.VMEM(s, F32) for s in scratch],
        compiler_params=pltpu.CompilerParams(vmem_limit_bytes=40 * 2**20),
        cost_estimate=pl.CostEstimate(flops=flops, bytes_accessed=moved, transcendentals=0),
    )(*args)


def swap(x):
    return lax.ppermute(x, "scan", [(0, 1), (1, 0)])


def shift(x, rows, cols):
    n_a, n_b = lax.axis_size("tx"), lax.axis_size("ty")
    route = [
        (a * n_b + b, (a + rows) * n_b + b + cols)
        for a in range(n_a)
        for b in range(n_b)
        if 0 <= a + rows < n_a and 0 <= b + cols < n_b
    ]
    return lax.ppermute(x, ("tx", "ty"), route)


def at(v, i):
    return lax.dynamic_index_in_dim(v, i, 0, keepdims=False)


def along(kind):
    def move(x, d):
        if kind == "x":
            route = [(i, ((i // 4 + d) % 4) * 4 + i % 4) for i in range(16)]
        else:
            route = [(i, (i // 4) * 4 + (i + d) % 4) for i in range(16)]
        return lax.ppermute(x, "ty", route)

    return move


def scatter_sum(v, index, n, move):
    got = [move(at(v, (index + d) % n), d) for d in range(1, n)]
    total = at(v, index)
    for g in got:
        total = total + g
    return total


def gather(v, index, n, move):
    got = [v] + [move(v, d) for d in range(1, n)]
    out = jnp.zeros((n,) + v.shape, v.dtype)
    for d, g in enumerate(got):
        out = lax.dynamic_update_index_in_dim(out, g, (index - d) % n, 0)
    return out


def sum_everywhere(grads, s):
    col = lax.axis_index("ty")
    x, y = col // 4, col % 4
    v = at(grads, s) + swap(at(grads, 1 - s))
    v = scatter_sum(v.reshape(4, 128, W), x, 4, along("x"))
    v = scatter_sum(v.reshape(4, 32, W), y, 4, along("y"))
    for bit in (1, 2, 4):
        v = v + lax.ppermute(v, "tx", [(i, i ^ bit) for i in range(8)])
    v = gather(v, y, 4, along("y")).reshape(128, W)
    v = gather(v, x, 4, along("x")).reshape(2, W, W)
    other = swap(v)
    return jnp.where(s == 0, jnp.stack([v, other]), jnp.stack([other, v]))


def body(object_slices, probe_modes, offsets, measured):
    s = lax.axis_index("scan").astype(jnp.int32)
    tab = jnp.asarray(tables())
    perm = jnp.asarray(deinterleave())

    halos = []
    for layer in range(2):
        plane = at(object_slices[layer], s)
        mine = (
            shift(plane[:W, :], -1, 0),
            shift(plane[:, :W], 0, -1),
            shift(plane[:W, :W], -1, -1),
        )
        halos.append(mine + tuple(swap(h) for h in mine))

    off = offsets.reshape(2)
    off_other = swap(off)
    scal = jnp.concatenate([off, s[None]])
    pair = jnp.concatenate([off, off_other])

    own, probe, meas = call(
        prep_kernel,
        [(2, 2, W, W), (2, 2, W, W), (W, W)],
        (off, object_slices, probe_modes, measured[0], perm),
        flops=12 * W**3,
    )
    obj0, back = call(
        first_kernel,
        [(2, W, W), (2, 2, W, W)],
        (scal, own[0], *halos[0], probe, tab),
        flops=48 * W**3,
    )
    grad1, wave = call(
        middle_kernel,
        [(2, W, W), (2, 2, W, W)],
        (scal, own[1], *halos[1], back, meas, tab),
        flops=96 * W**3,
        scratch=[(2, W, W), (2, 2, W, W)],
    )
    grad0, grad_probe = call(
        last_kernel,
        [(2, W, W), (2, 2, W, W)],
        (scal, wave, obj0, probe, tab),
        flops=48 * W**3,
    )

    def out(grad):
        own_sum, below, right, diag = call(
            spread_kernel,
            [(2 * W, 2 * W), (W, 2 * W), (2 * W, W), (W, W)],
            (pair, at(grad, s), swap(at(grad, 1 - s))),
        )
        mine = (shift(below, 1, 0), shift(right, 0, 1), shift(diag, 1, 1))
        other = tuple(swap(h) for h in mine)
        return call(
            finish_kernel,
            [(2, 2 * W, 2 * W)],
            (s[None], own_sum, *mine, swap(own_sum), *other),
        )[0]

    tile1 = out(grad1)
    tile0 = out(grad0)
    return jnp.stack([tile0, tile1]), sum_everywhere(grad_probe, s)


def solution(mesh):
    placed = (
        P(None, None, "tx", "ty"),
        P(),
        P(("tx", "ty", "scan"), None),
        P(("tx", "ty", "scan"), None, None),
    )
    return jax.shard_map(
        body,
        mesh=mesh,
        in_specs=placed,
        out_specs=(P(None, None, "tx", "ty"), P()),
        check_vma=False,
    )
```

time: 658 us -> 193 us (0.29)
  the two profiles are of different devices: /device:TPU:57 before, /device:TPU:7 now
where the time goes in v1:
time: 193 us; the launch traced here: 192 us
  starting transfers between devices  75.9 us (39%)
  waiting for transfers between devices  65.4 us (34%)
  local copies, waits for them, and re-layouts  23.5 us (12%)
  Pallas kernels  19 us (10%)
  other arithmetic  7.12 us (4%)
    ppermute x12, waiting for transfers between devices, shift(): return lax.ppermute(x, ('tx', 'ty'), route)  34.7 us
    ppermute x12, starting transfers between devices, shift(): return lax.ppermute(x, ('tx', 'ty'), route)  30.6 us
    ppermute x12, waiting for transfers between devices, move(): return lax.ppermute(x, 'ty', route)  23.2 us
    ppermute x19, starting transfers between devices, swap(): return lax.ppermute(x, 'scan', [(0, 1), (1, 0)])  22.9 us
    pallas_call x8, Pallas kernels, call(): pl.pallas_call(kernel, out_shape=[jax.ShapeDtypeStruct(o, F32) for o in o...  19 us
    ppermute x12, starting transfers between devices, move(): return lax.ppermute(x, 'ty', route)  11.7 us
    ppermute x3, starting transfers between devices, sum_everywhere(): v = v + lax.ppermute(v, 'tx', [(i, i ^ bit) for i in range(8)])  10.7 us
    unnamed x50, local copies, waits for them, and re-layouts  10.5 us
  transfers between devices with their start and end apart: 46, of which 12 were waited for; matrix products, arithmetic and copies ran while one was open for 6% of the time, Pallas kernels for 6%

profile of v1, /device:TPU:7, one launch (start us, length us, event | category | flops | bytes accessed | tf_op | source)
XLA Modules:
  0.0 192.2 jit_solution(12226676833098323314)
XLA Ops:
  0.6 4.0 %fusion.4 = (f32[1,2,512,512]{3,2,1,0:T(8,128)}, f32[1,2,512,512]{3,2,1,0:T(8,128)S(1)}) fusion(f32[2,2,512,512]{3,2,1,0:T(8,128)} %obj.1), kind=kLoop, calls=%fused_computation.36 | loop fusion | bytes 8388608 | tf_op jit(solution)/shard_map/slice | solution.py:345
  7.5 5.2 %collective-permute-start.2 = (f32[512,256]{1,0:T(8,128)S(1)}, f32[512,256]{1,0:T(8,128)}, u32[]{:S(2)}, u32[]{:S(2)}) collective-permute-start(f32[512,256]{1,0:T(8,128)S(1)} %slice.48), channel_id=1, source_target_pairs={{2,0},{4,2},{6,4},{8,6},{10,8},{12,10},{14,12},{16,14},{18,16},{20... | collective-permute-start | bytes 1572872 | tf_op jit(solution)/shard_map/ppermute | solution.py:290
  12.7 2.4 %collective-permute-start.8 = (f32[512,256]{1,0:T(8,128)S(1)}, f32[512,256]{1,0:T(8,128)}, u32[]{:S(2)}, u32[]{:S(2)}) collective-permute-start(f32[512,256]{1,0:T(8,128)S(1)} %slice.50), channel_id=1, source_target_pairs={{2,0},{4,2},{6,4},{8,6},{10,8},{12,10},{14,12},{16,14},{18,16},{20... | collective-permute-start | bytes 1572872 | tf_op jit(solution)/shard_map/ppermute | solution.py:290
  20.1 28.6 %collective-permute-done.3.d0 = f32[256,256]{1,0:T(8,128)} collective-permute-done((f32[256,256]{1,0:T(8,128)S(1)}, f32[256,256]{1,0:T(8,128)}, u32[]{:S(2)}, u32[]{:S(2)}) %collective-permute-start.3) | collective-permute-done | bytes 262176 | tf_op jit(solution)/shard_map/ppermute | solution.py:290
  58.5 3.4 %shard_map.78 = (f32[2,256,256]{2,1,0:T(8,128)S(1)}, f32[2,2,256,256]{3,2,1,0:T(8,128)S(1)}) custom-call(s32[3]{0:T(128)S(1)} %pad_add_fusion.1.scal, f32[2,256,256]{2,1,0:T(8,128)S(1)} %copy-done.2, f32[256,512]{1,0:T(8,128)} %collective-permute-done.7.b0, f32[512,256]{1,0:T(8,128)} %collective-permute-done.8.r0, f32[256,256]{1,0:T(8,128)S(1)} %collective-permute-done.9.d0, ...), custom_call_target="tpu_custom_call" | custom-call | flops 805306368 | bytes 7864332 | tf_op jit(solution)/shard_map/pallas_call | solution.py:267
  61.9 4.8 %shard_map.79 = (f32[2,256,256]{2,1,0:T(8,128)S(1)}, f32[2,2,256,256]{3,2,1,0:T(8,128)S(1)}) custom-call(s32[3]{0:T(128)S(1)} %pad_add_fusion.1.scal, f32[2,256,256]{2,1,0:T(8,128)S(1)} %copy-done.3, f32[256,512]{1,0:T(8,128)} %collective-permute-done.1.b0, f32[512,256]{1,0:T(8,128)} %collective-permute-done.2.r0, f32[256,256]{1,0:T(8,128)} %collective-permute-done.3.d0, ...), custom_call_target="tpu_custom_call" | custom-call | flops 1610612736 | bytes 8126476 | tf_op jit(solution)/shard_map/pallas_call | solution.py:267
  85.6 2.4 %collective-permute-start.13 = (f32[256,256]{1,0:T(8,128)S(1)}, f32[256,256]{1,0:T(8,128)S(1)}, u32[]{:S(2)}, u32[]{:S(2)}) collective-permute-start(f32[256,256]{1,0:T(8,128)S(1)} %get-tuple-element.45), channel_id=1, source_target_pairs={{0,1},{1,0},{2,3},{3,2},{4,5},{5,4},{6,7},{7,6},{8,9},{9,8},{10,11... | collective-permute-start | bytes 786440 | tf_op jit(solution)/shard_map/ppermute | solution.py:279
  89.9 4.4 %collective-permute-start.24 = (f32[256,256]{1,0:T(8,128)S(1)}, f32[256,256]{1,0:T(8,128)S(1)}, u32[]{:S(2)}, u32[]{:S(2)}) collective-permute-start(f32[256,256]{1,0:T(8,128)S(1)} %get-tuple-element.34), channel_id=1, source_target_pairs={{0,34},{2,36},{4,38},{6,40},{8,42},{10,44},{12,46},{14,48},{16,50}... | collective-permute-start | bytes 786440 | tf_op jit(solution)/shard_map/ppermute | solution.py:290
  96.0 4.7 %collective-permute-done.36 = f32[32,256]{1,0:T(8,128)S(1)} collective-permute-done((f32[32,256]{1,0:T(8,128)S(1)}, f32[32,256]{1,0:T(8,128)S(1)}, u32[]{:S(2)}, u32[]{:S(2)}) %collective-permute-start.36) | collective-permute-done | bytes 32800 | tf_op jit(solution)/shard_map/ppermute | solution.py:331
  100.6 4.3 %collective-permute-start.37 = (f32[32,256]{1,0:T(8,128)S(1)}, f32[32,256]{1,0:T(8,128)S(1)}, u32[]{:S(2)}, u32[]{:S(2)}) collective-permute-start(f32[32,256]{1,0:T(8,128)S(1)} %add.199), channel_id=1, source_target_pairs={{0,64},{32,96},{64,0},{96,32},{128,192},{160,224},{192,128},{224,1... | collective-permute-start | bytes 98312 | tf_op jit(solution)/shard_map/ppermute | solution.py:331
  106.2 4.8 %collective-permute-start.38 = (f32[32,256]{1,0:T(8,128)S(1)}, f32[32,256]{1,0:T(8,128)S(1)}, u32[]{:S(2)}, u32[]{:S(2)}) collective-permute-start(f32[32,256]{1,0:T(8,128)S(1)} %add.200), channel_id=1, source_target_pairs={{0,128},{32,160},{64,192},{96,224},{128,0},{160,32},{192,64},{224,... | collective-permute-start | bytes 98312 | tf_op jit(solution)/shard_map/ppermute | solution.py:331
  113.8 4.8 %collective-permute-start.16 = (f32[256,256]{1,0:T(8,128)S(1)}, f32[256,256]{1,0:T(8,128)S(1)}, u32[]{:S(2)}, u32[]{:S(2)}) collective-permute-start(f32[256,256]{1,0:T(8,128)S(1)} %get-tuple-element.29), channel_id=1, source_target_pairs={{0,34},{2,36},{4,38},{6,40},{8,42},{10,44},{12,46},{14,48},{16,50}... | collective-permute-start | bytes 786440 | tf_op jit(solution)/shard_map/ppermute | solution.py:290
  118.6 2.6 %collective-permute-start.28 = (f32[256,256]{1,0:T(8,128)S(1)}, f32[256,256]{1,0:T(8,128)}, u32[]{:S(2)}, u32[]{:S(2)}) collective-permute-start(f32[256,256]{1,0:T(8,128)S(1)} %collective-permute-done.24.d0), channel_id=1, source_target_pairs={{0,1},{1,0},{2,3},{3,2},{4,5},{5,4},{6,7},{7,6},{8,9},{9,8},{10,11... | collective-permute-start | bytes 786440 | tf_op jit(solution)/shard_map/ppermute | solution.py:279
  122.1 2.4 %collective-permute-start.22 = (f32[256,512]{1,0:T(8,128)}, f32[256,512]{1,0:T(8,128)}, u32[]{:S(2)}, u32[]{:S(2)}) collective-permute-start(f32[256,512]{1,0:T(8,128)} %get-tuple-element.32), channel_id=1, source_target_pairs={{0,32},{2,34},{4,36},{6,38},{8,40},{10,42},{12,44},{14,46},{16,48}... | collective-permute-start | bytes 1572872 | tf_op jit(solution)/shard_map/ppermute | solution.py:290
  128.3 2.7 %collective-permute-start.40 = (f32[32,256]{1,0:T(8,128)}, f32[32,256]{1,0:T(8,128)S(1)}, u32[]{:S(2)}, u32[]{:S(2)}) collective-permute-start(f32[32,256]{1,0:T(8,128)} %get-tuple-element.37), channel_id=1, source_target_pairs={{0,4},{2,6},{4,0},{6,2},{8,12},{10,14},{12,8},{14,10},{16,20},{18,... | collective-permute-start | bytes 98312 | tf_op jit(solution)/shard_map/ppermute | solution.py:303
  131.7 10.6 %collective-permute-done.40 = f32[32,256]{1,0:T(8,128)S(1)} collective-permute-done((f32[32,256]{1,0:T(8,128)}, f32[32,256]{1,0:T(8,128)S(1)}, u32[]{:S(2)}, u32[]{:S(2)}) %collective-permute-start.40) | collective-permute-done | bytes 32800 | tf_op jit(solution)/shard_map/ppermute | solution.py:303
  147.4 2.3 %collective-permute-start.17 = (f32[512,512]{1,0:T(8,128)S(1)}, f32[512,512]{1,0:T(8,128)}, u32[]{:S(2)}, u32[]{:S(2)}) collective-permute-start(f32[512,512]{1,0:T(8,128)S(1)} %get-tuple-element.26.own0), channel_id=1, source_target_pairs={{0,1},{1,0},{2,3},{3,2},{4,5},{5,4},{6,7},{7,6},{8,9},{9,8},{10,11... | collective-permute-start | bytes 3145736 | tf_op jit(solution)/shard_map/ppermute | solution.py:279
  153.4 2.8 %collective-permute-start.26 = (f32[256,512]{1,0:T(8,128)}, f32[256,512]{1,0:T(8,128)S(1)}, u32[]{:S(2)}, u32[]{:S(2)}) collective-permute-start(f32[256,512]{1,0:T(8,128)} %collective-permute-done.22.b0), channel_id=1, source_target_pairs={{0,1},{1,0},{2,3},{3,2},{4,5},{5,4},{6,7},{7,6},{8,9},{9,8},{10,11... | collective-permute-start | bytes 1572872 | tf_op jit(solution)/shard_map/ppermute | solution.py:279
  156.2 4.0 %collective-permute-done.15.r0 = f32[512,256]{1,0:T(8,128)} collective-permute-done((f32[512,256]{1,0:T(8,128)}, f32[512,256]{1,0:T(8,128)}, u32[]{:S(2)}, u32[]{:S(2)}) %collective-permute-start.15) | collective-permute-done | bytes 524320 | tf_op jit(solution)/shard_map/ppermute | solution.py:290
  160.2 4.4 %collective-permute-start.27 = (f32[512,256]{1,0:T(8,128)}, f32[512,256]{1,0:T(8,128)S(1)}, u32[]{:S(2)}, u32[]{:S(2)}) collective-permute-start(f32[512,256]{1,0:T(8,128)} %collective-permute-done.23.r0), channel_id=1, source_target_pairs={{0,1},{1,0},{2,3},{3,2},{4,5},{5,4},{6,7},{7,6},{8,9},{9,8},{10,11... | collective-permute-start | bytes 1572872 | tf_op jit(solution)/shard_map/ppermute | solution.py:279
  167.8 3.4 %collective-permute-done.43 = f32[128,256]{1,0:T(8,128)S(1)} collective-permute-done((f32[128,256]{1,0:T(8,128)S(1)}, f32[128,256]{1,0:T(8,128)S(1)}, u32[]{:S(2)}, u32[]{:S(2)}) %collective-permute-start.43) | collective-permute-done | bytes 131104 | tf_op jit(solution)/shard_map/ppermute | solution.py:303
  172.2 4.5 %collective-permute-done.44 = f32[128,256]{1,0:T(8,128)S(1)} collective-permute-done((f32[128,256]{1,0:T(8,128)S(1)}, f32[128,256]{1,0:T(8,128)S(1)}, u32[]{:S(2)}, u32[]{:S(2)}) %collective-permute-start.44) | collective-permute-done | bytes 131104 | tf_op jit(solution)/shard_map/ppermute | solution.py:303
  187.0 2.5 %pad_maximum_fusion = f32[2,2,512,512]{3,2,1,0:T(8,128)} fusion(f32[1,2,512,512]{3,2,1,0:T(8,128)S(1)} %bitcast.76, f32[1,2,512,512]{3,2,1,0:T(8,128)S(1)} %bitcast.77), kind=kLoop, calls=%fused_computation | loop fusion | flops 1048576 | bytes 8388608 | tf_op jit(solution)/shard_map/stack | solution.py:400
  189.4 2.7 %maximum_select_fusion = f32[2,2,256,256]{3,2,1,0:T(8,128)} fusion(f32[1,2,256,256]{3,2,1,0:T(8,128)} %bitcast.38, f32[1,2,256,256]{3,2,1,0:T(8,128)} %bitcast.36, pred[]{:T(512)S(6)} %eq.19), kind=kLoop, calls=%fused_computation.1 | loop fusion | flops 786432 | bytes 2097153 | tf_op jit(solution)/shard_map/jit(_where)/select_n | solution.py:335
  (160 shorter events, 72.5 us)
Async XLA Ops:
  6.0 12.9 %collective-permute-start.9 = (f32[256,256]{1,0:T(8,128)S(1)}, f32[256,256]{1,0:T(8,128)S(1)}, u32[]{:S(2)}, u32[]{:S(2)}) collective-permute-start(f32[256,256]{1,0:T(8,128)S(1)} %slice.51), channel_id=1, source_target_pairs={{34,0},{36,2},{38,4},{40,6},{42,8},{44,10},{46,12},{48,14},{50,16}... | collective-permute-start | bytes 786440 | tf_op jit(solution)/shard_map/ppermute | solution.py:290
  7.5 43.9 %collective-permute-start.2 = (f32[512,256]{1,0:T(8,128)S(1)}, f32[512,256]{1,0:T(8,128)}, u32[]{:S(2)}, u32[]{:S(2)}) collective-permute-start(f32[512,256]{1,0:T(8,128)S(1)} %slice.48), channel_id=1, source_target_pairs={{2,0},{4,2},{6,4},{8,6},{10,8},{12,10},{14,12},{16,14},{18,16},{20... | collective-permute-start | bytes 1572872 | tf_op jit(solution)/shard_map/ppermute | solution.py:290
  12.7 38.2 %collective-permute-start.8 = (f32[512,256]{1,0:T(8,128)S(1)}, f32[512,256]{1,0:T(8,128)}, u32[]{:S(2)}, u32[]{:S(2)}) collective-permute-start(f32[512,256]{1,0:T(8,128)S(1)} %slice.50), channel_id=1, source_target_pairs={{2,0},{4,2},{6,4},{8,6},{10,8},{12,10},{14,12},{16,14},{18,16},{20... | collective-permute-start | bytes 1572872 | tf_op jit(solution)/shard_map/ppermute | solution.py:290
  16.2 34.7 %collective-permute-start.7 = (f32[256,512]{1,0:T(8,128)S(1)}, f32[256,512]{1,0:T(8,128)}, u32[]{:S(2)}, u32[]{:S(2)}) collective-permute-start(f32[256,512]{1,0:T(8,128)S(1)} %dynamic-slice_bitcast_fusion.2), channel_id=1, source_target_pairs={{32,0},{34,2},{36,4},{38,6},{40,8},{42,10},{44,12},{46,14},{48,16}... | collective-permute-start | bytes 1572872 | tf_op jit(solution)/shard_map/ppermute | solution.py:290
  17.5 34.0 %collective-permute-start.1 = (f32[256,512]{1,0:T(8,128)S(1)}, f32[256,512]{1,0:T(8,128)}, u32[]{:S(2)}, u32[]{:S(2)}) collective-permute-start(f32[256,512]{1,0:T(8,128)S(1)} %dynamic-slice_bitcast_fusion.3), channel_id=1, source_target_pairs={{32,0},{34,2},{36,4},{38,6},{40,8},{42,10},{44,12},{46,14},{48,16}... | collective-permute-start | bytes 1572872 | tf_op jit(solution)/shard_map/ppermute | solution.py:290
  18.8 29.9 %collective-permute-start.3 = (f32[256,256]{1,0:T(8,128)S(1)}, f32[256,256]{1,0:T(8,128)}, u32[]{:S(2)}, u32[]{:S(2)}) collective-permute-start(f32[256,256]{1,0:T(8,128)S(1)} %slice.49), channel_id=1, source_target_pairs={{34,0},{36,2},{38,4},{40,6},{42,8},{44,10},{46,12},{48,14},{50,16}... | collective-permute-start | bytes 786440 | tf_op jit(solution)/shard_map/ppermute | solution.py:290
  76.0 12.0 %collective-permute-start.21 = (f32[256,256]{1,0:T(8,128)S(1)}, f32[256,256]{1,0:T(8,128)S(1)}, u32[]{:S(2)}, u32[]{:S(2)}) collective-permute-start(f32[256,256]{1,0:T(8,128)S(1)} %get-tuple-element.47), channel_id=1, source_target_pairs={{0,1},{1,0},{2,3},{3,2},{4,5},{5,4},{6,7},{7,6},{8,9},{9,8},{10,11... | collective-permute-start | bytes 786440 | tf_op jit(solution)/shard_map/ppermute | solution.py:279
  82.1 12.2 %collective-permute-start.33 = (f32[32,256]{1,0:T(8,128)S(1)}, f32[32,256]{1,0:T(8,128)S(1)}, u32[]{:S(2)}, u32[]{:S(2)}) collective-permute-start(f32[32,256]{1,0:T(8,128)S(1)} %get-tuple-element.49), channel_id=1, source_target_pairs={{0,2},{2,4},{4,6},{6,0},{8,10},{10,12},{12,14},{14,8},{16,18},{18,... | collective-permute-start | bytes 98312 | tf_op jit(solution)/shard_map/ppermute | solution.py:303
  83.1 11.2 %collective-permute-start.35 = (f32[32,256]{1,0:T(8,128)S(1)}, f32[32,256]{1,0:T(8,128)S(1)}, u32[]{:S(2)}, u32[]{:S(2)}) collective-permute-start(f32[32,256]{1,0:T(8,128)S(1)} %get-tuple-element.50), channel_id=1, source_target_pairs={{0,6},{2,0},{4,2},{6,4},{8,14},{10,8},{12,10},{14,12},{16,22},{18,... | collective-permute-start | bytes 98312 | tf_op jit(solution)/shard_map/ppermute | solution.py:303
  85.6 25.5 %collective-permute-start.13 = (f32[256,256]{1,0:T(8,128)S(1)}, f32[256,256]{1,0:T(8,128)S(1)}, u32[]{:S(2)}, u32[]{:S(2)}) collective-permute-start(f32[256,256]{1,0:T(8,128)S(1)} %get-tuple-element.45), channel_id=1, source_target_pairs={{0,1},{1,0},{2,3},{3,2},{4,5},{5,4},{6,7},{7,6},{8,9},{9,8},{10,11... | collective-permute-start | bytes 786440 | tf_op jit(solution)/shard_map/ppermute | solution.py:279
  89.9 28.7 %collective-permute-start.24 = (f32[256,256]{1,0:T(8,128)S(1)}, f32[256,256]{1,0:T(8,128)S(1)}, u32[]{:S(2)}, u32[]{:S(2)}) collective-permute-start(f32[256,256]{1,0:T(8,128)S(1)} %get-tuple-element.34), channel_id=1, source_target_pairs={{0,34},{2,36},{4,38},{6,40},{8,42},{10,44},{12,46},{14,48},{16,50}... | collective-permute-start | bytes 786440 | tf_op jit(solution)/shard_map/ppermute | solution.py:290
  106.2 14.9 %collective-permute-start.38 = (f32[32,256]{1,0:T(8,128)S(1)}, f32[32,256]{1,0:T(8,128)S(1)}, u32[]{:S(2)}, u32[]{:S(2)}) collective-permute-start(f32[32,256]{1,0:T(8,128)S(1)} %add.200), channel_id=1, source_target_pairs={{0,128},{32,160},{64,192},{96,224},{128,0},{160,32},{192,64},{224,... | collective-permute-start | bytes 98312 | tf_op jit(solution)/shard_map/ppermute | solution.py:331
  113.8 12.9 %collective-permute-start.16 = (f32[256,256]{1,0:T(8,128)S(1)}, f32[256,256]{1,0:T(8,128)S(1)}, u32[]{:S(2)}, u32[]{:S(2)}) collective-permute-start(f32[256,256]{1,0:T(8,128)S(1)} %get-tuple-element.29), channel_id=1, source_target_pairs={{0,34},{2,36},{4,38},{6,40},{8,42},{10,44},{12,46},{14,48},{16,50}... | collective-permute-start | bytes 786440 | tf_op jit(solution)/shard_map/ppermute | solution.py:290
  122.1 24.4 %collective-permute-start.22 = (f32[256,512]{1,0:T(8,128)}, f32[256,512]{1,0:T(8,128)}, u32[]{:S(2)}, u32[]{:S(2)}) collective-permute-start(f32[256,512]{1,0:T(8,128)} %get-tuple-element.32), channel_id=1, source_target_pairs={{0,32},{2,34},{4,36},{6,38},{8,40},{10,42},{12,44},{14,46},{16,48}... | collective-permute-start | bytes 1572872 | tf_op jit(solution)/shard_map/ppermute | solution.py:290
  124.5 23.0 %collective-permute-start.23 = (f32[512,256]{1,0:T(8,128)}, f32[512,256]{1,0:T(8,128)}, u32[]{:S(2)}, u32[]{:S(2)}) collective-permute-start(f32[512,256]{1,0:T(8,128)} %get-tuple-element.33), channel_id=1, source_target_pairs={{0,2},{2,4},{4,6},{6,8},{8,10},{10,12},{12,14},{14,16},{16,18},{18... | collective-permute-start | bytes 1572872 | tf_op jit(solution)/shard_map/ppermute | solution.py:290
  127.4 50.9 %collective-permute-start.25 = (f32[512,512]{1,0:T(8,128)S(1)}, f32[512,512]{1,0:T(8,128)S(1)}, u32[]{:S(2)}, u32[]{:S(2)}) collective-permute-start(f32[512,512]{1,0:T(8,128)S(1)} %get-tuple-element.31.own0), channel_id=1, source_target_pairs={{0,1},{1,0},{2,3},{3,2},{4,5},{5,4},{6,7},{7,6},{8,9},{9,8},{10,11... | collective-permute-start | bytes 3145736 | tf_op jit(solution)/shard_map/ppermute | solution.py:279
  128.3 14.0 %collective-permute-start.40 = (f32[32,256]{1,0:T(8,128)}, f32[32,256]{1,0:T(8,128)S(1)}, u32[]{:S(2)}, u32[]{:S(2)}) collective-permute-start(f32[32,256]{1,0:T(8,128)} %get-tuple-element.37), channel_id=1, source_target_pairs={{0,4},{2,6},{4,0},{6,2},{8,12},{10,14},{12,8},{14,10},{16,20},{18,... | collective-permute-start | bytes 98312 | tf_op jit(solution)/shard_map/ppermute | solution.py:303
  131.0 13.6 %collective-permute-start.41 = (f32[32,256]{1,0:T(8,128)}, f32[32,256]{1,0:T(8,128)S(1)}, u32[]{:S(2)}, u32[]{:S(2)}) collective-permute-start(f32[32,256]{1,0:T(8,128)} %get-tuple-element.37), channel_id=1, source_target_pairs={{0,6},{2,0},{4,2},{6,4},{8,14},{10,8},{12,10},{14,12},{16,22},{18,... | collective-permute-start | bytes 98312 | tf_op jit(solution)/shard_map/ppermute | solution.py:303
  142.3 11.1 %collective-permute-start.14 = (f32[256,512]{1,0:T(8,128)}, f32[256,512]{1,0:T(8,128)}, u32[]{:S(2)}, u32[]{:S(2)}) collective-permute-start(f32[256,512]{1,0:T(8,128)} %copy-done.24), channel_id=1, source_target_pairs={{0,32},{2,34},{4,36},{6,38},{8,40},{10,42},{12,44},{14,46},{16,48}... | collective-permute-start | bytes 1572872 | tf_op jit(solution)/shard_map/ppermute | solution.py:290
  144.5 15.6 %collective-permute-start.15 = (f32[512,256]{1,0:T(8,128)}, f32[512,256]{1,0:T(8,128)}, u32[]{:S(2)}, u32[]{:S(2)}) collective-permute-start(f32[512,256]{1,0:T(8,128)} %copy-done.23), channel_id=1, source_target_pairs={{0,2},{2,4},{4,6},{6,8},{8,10},{10,12},{12,14},{14,16},{16,18},{18... | collective-permute-start | bytes 1572872 | tf_op jit(solution)/shard_map/ppermute | solution.py:290
  146.5 18.1 %collective-permute-start.42 = (f32[128,256]{1,0:T(8,128)S(1)}, f32[128,256]{1,0:T(8,128)}, u32[]{:S(2)}, u32[]{:S(2)}) collective-permute-start(f32[128,256]{1,0:T(8,128)S(1)} %bitcast.87), channel_id=1, source_target_pairs={{0,8},{2,10},{4,12},{6,14},{8,16},{10,18},{12,20},{14,22},{16,24},... | collective-permute-start | bytes 393224 | tf_op jit(solution)/shard_map/ppermute | solution.py:303
  147.4 37.4 %collective-permute-start.17 = (f32[512,512]{1,0:T(8,128)S(1)}, f32[512,512]{1,0:T(8,128)}, u32[]{:S(2)}, u32[]{:S(2)}) collective-permute-start(f32[512,512]{1,0:T(8,128)S(1)} %get-tuple-element.26.own0), channel_id=1, source_target_pairs={{0,1},{1,0},{2,3},{3,2},{4,5},{5,4},{6,7},{7,6},{8,9},{9,8},{10,11... | collective-permute-start | bytes 3145736 | tf_op jit(solution)/shard_map/ppermute | solution.py:279
  153.4 25.6 %collective-permute-start.26 = (f32[256,512]{1,0:T(8,128)}, f32[256,512]{1,0:T(8,128)S(1)}, u32[]{:S(2)}, u32[]{:S(2)}) collective-permute-start(f32[256,512]{1,0:T(8,128)} %collective-permute-done.22.b0), channel_id=1, source_target_pairs={{0,1},{1,0},{2,3},{3,2},{4,5},{5,4},{6,7},{7,6},{8,9},{9,8},{10,11... | collective-permute-start | bytes 1572872 | tf_op jit(solution)/shard_map/ppermute | solution.py:279
  160.2 20.2 %collective-permute-start.27 = (f32[512,256]{1,0:T(8,128)}, f32[512,256]{1,0:T(8,128)S(1)}, u32[]{:S(2)}, u32[]{:S(2)}) collective-permute-start(f32[512,256]{1,0:T(8,128)} %collective-permute-done.23.r0), channel_id=1, source_target_pairs={{0,1},{1,0},{2,3},{3,2},{4,5},{5,4},{6,7},{7,6},{8,9},{9,8},{10,11... | collective-permute-start | bytes 1572872 | tf_op jit(solution)/shard_map/ppermute | solution.py:279
  (47 other events, 417.4 us)

commit v2 on v1

--- a/solution.py
+++ b/solution.py
@@ -150,11 +150,10 @@
             probe_out[m, p] = pltpu.roll(x, tc, 1)
 
     def exact(x):
-        hi, rest = x.astype(B16), None
+        hi = x.astype(B16)
         rest = x - hi.astype(F32)
         mid = rest.astype(B16)
-        low = (rest - mid.astype(F32)).astype(B16)
-        return hi, mid, low
+        return hi, mid, (rest - mid.astype(F32)).astype(B16)
 
     hi, mid, low = exact(meas[...])
     x = dot(perm[0], hi) + dot(perm[0], mid) + dot(perm[0], low)
@@ -175,29 +174,27 @@
     return jnp.where(halo_c, jnp.where(halo_r, diag[...], right_v), out)
 
 
-def patch_planes(scal, own, halo_mine, halo_other, out):
-    s = scal[2]
-    out[s] = whole_patch(scal, own[s], *halo_mine)
-    out[1 - s] = whole_patch(scal, own[1 - s], *halo_other)
-
-
-def first_kernel(scal, own, b0, r0, d0, b1, r1, d1, probe, tab, obj_out, back_out):
-    patch_planes(scal, own, (b0, r0, d0), (b1, r1, d1), obj_out)
-    o_r, o_i = obj_out[0], obj_out[1]
-    for m in range(2):
-        re, im = cmul(probe[m, 0], probe[m, 1], o_r, o_i)
-        re, im = both_axes(tab, "prop", re, im)
-        back_out[m, 0] = re
-        back_out[m, 1] = im
-
-
-def middle_kernel(scal, own, b0, r0, d0, b1, r1, d1, back, meas, tab, grad_out, wave_out, obj, far):
-    patch_planes(scal, own, (b0, r0, d0), (b1, r1, d1), obj)
-    for m in range(2):
-        re, im = cmul(back[m, 0], back[m, 1], obj[0], obj[1])
-        re, im = both_axes(tab, "fwd", re, im)
-        far[m, 0] = re
-        far[m, 1] = im
+def put_pair(s, first, second, keep_out, send_out):
+    keep_out[...] = jnp.where(s == 0, first, second)
+    send_out[...] = jnp.where(s == 0, second, first)
+
+
+def gradient_kernel(
+    scal, own, b0, r0, d0, b1, r1, d1, probe, meas, tab,
+    keep_out, send_out, probe_keep_out, probe_send_out,
+    obj, back, far, modes,
+):
+    s, tr, tc = scal[2], scal[0] % W, scal[1] % W
+    for layer in range(2):
+        for plane, halo in ((s, (b0, r0, d0)), (1 - s, (b1, r1, d1))):
+            parts = [h.at[layer] for h in halo]
+            obj[layer, plane] = whole_patch(scal, own[layer, plane], *parts)
+    for m in range(2):
+        re, im = cmul(probe[m, 0], probe[m, 1], obj[0, 0], obj[0, 1])
+        back[m, 0], back[m, 1] = both_axes(tab, "prop", re, im)
+    for m in range(2):
+        re, im = cmul(back[m, 0], back[m, 1], obj[1, 0], obj[1, 1])
+        far[m, 0], far[m, 1] = both_axes(tab, "fwd", re, im)
     inten = far[0, 0] ** 2 + far[0, 1] ** 2 + far[1, 0] ** 2 + far[1, 1] ** 2
     resid = 2.0 * (inten - meas[...])
     g_r = g_i = None
@@ -205,26 +202,21 @@
         re, im = both_axes(tab, "inv", resid * far[m, 0], resid * far[m, 1])
         a, b = cmul_conj(back[m, 0], back[m, 1], re, im)
         g_r, g_i = (a, b) if g_r is None else (g_r + a, g_i + b)
-        wave_out[m, 0], wave_out[m, 1] = cmul_conj(obj[0], obj[1], re, im)
-    grad_out[0] = g_r
-    grad_out[1] = g_i
-
-
-def last_kernel(scal, wave, obj, probe, tab, grad_out, probe_out):
-    tr, tc = scal[0] % W, scal[1] % W
+        modes[m, 0], modes[m, 1] = cmul_conj(obj[1, 0], obj[1, 1], re, im)
+    put_pair(s, g_r, g_i, keep_out.at[1], send_out.at[1])
     g_r = g_i = None
     for m in range(2):
-        re, im = both_axes(tab, "back", wave[m, 0], wave[m, 1])
+        re, im = both_axes(tab, "back", modes[m, 0], modes[m, 1])
         a, b = cmul_conj(probe[m, 0], probe[m, 1], re, im)
         g_r, g_i = (a, b) if g_r is None else (g_r + a, g_i + b)
-        for p, x in enumerate(cmul_conj(obj[0], obj[1], re, im)):
+        for p, x in enumerate(cmul_conj(obj[0, 0], obj[0, 1], re, im)):
             x = pltpu.roll(x * (1.0 / 256.0), (W - tr) % W, 0)
-            probe_out[m, p] = pltpu.roll(x, (W - tc) % W, 1)
-    grad_out[0] = g_r
-    grad_out[1] = g_i
-
-
-def spread_kernel(scal, mine, other, own_out, below_out, right_out, diag_out):
+            modes[m, p] = pltpu.roll(x, (W - tc) % W, 1)
+    put_pair(s, g_r, g_i, keep_out.at[0], send_out.at[0])
+    put_pair(s, modes[0], modes[1], probe_keep_out, probe_send_out)
+
+
+def spread_kernel(scal, mine, other, own_out, below_out, right0, right1, diag_out):
     rho, gam = iotas()
 
     def band(index, q, t, i):
@@ -236,29 +228,40 @@
         rows = [band(rho, r // W, r % W, i) for i in range(3)]
         cols = [band(gam, c // W, c % W, j) for j in range(3)]
         where.append((rows, cols))
-    a, b = mine[...], other[...]
     for i in range(3):
         for j in range(3):
-            v = jnp.where(where[0][0][i] & where[0][1][j], a, 0.0) + jnp.where(
-                where[1][0][i] & where[1][1][j], b, 0.0
-            )
-            if i < 2 and j < 2:
-                own_out[i * W : (i + 1) * W, j * W : (j + 1) * W] = v
-            elif i < 2:
-                right_out[i * W : (i + 1) * W, :] = v
-            elif j < 2:
-                below_out[:, j * W : (j + 1) * W] = v
-            else:
-                diag_out[...] = v
-
-
-def finish_kernel(scal, own0, b0, r0, d0, own1, b1, r1, d1, out):
+            here = [r[i] & c[j] for r, c in where]
+            for k in range(2):
+                v = jnp.where(here[0], mine[k], 0.0) + jnp.where(here[1], other[k], 0.0)
+                if i < 2 and j < 2:
+                    own_out[k, i * W : (i + 1) * W, j * W : (j + 1) * W] = v
+                elif i < 2:
+                    (right0, right1)[k][i * W : (i + 1) * W, :] = v
+                elif j < 2:
+                    below_out[k, :, j * W : (j + 1) * W] = v
+                else:
+                    diag_out[k] = v
+
+
+def finish_kernel(scal, own0, b0, r00, r01, d0, own1, b1, r10, r11, d1, out):
     s = scal[0]
-    for plane, own, b, r, d in ((s, own0, b0, r0, d0), (1 - s, own1, b1, r1, d1)):
-        out[plane, W:, W:] = own[W:, W:]
-        out[plane, :W, :W] = own[:W, :W] + (b[:, :W] + r[:W, :] + d[...])
-        out[plane, :W, W:] = own[:W, W:] + b[:, W:]
-        out[plane, W:, :W] = own[W:, :W] + r[W:, :]
+    for k in range(2):
+        mine = (own0, b0, (r00, r01)[k], d0)
+        other = (own1, b1, (r10, r11)[k], d1)
+        for plane, (own, b, r, d) in ((s, mine), (1 - s, other)):
+            out[k, plane, W:, W:] = own[k, W:, W:]
+            out[k, plane, :W, :W] = own[k, :W, :W] + (b[k, :, :W] + r[:W, :] + d[k])
+            out[k, plane, :W, W:] = own[k, :W, W:] + b[k, :, W:]
+            out[k, plane, W:, :W] = own[k, W:, :W] + r[W:, :]
+
+
+def place_kernel(scal, *refs):
+    parts, out = refs[:-1], refs[-1]
+    for d, part in enumerate(parts):
+        out[scal[0] ^ d] = part[...]
+
+
+LIMIT = 8 * 2**20
 
 
 def call(kernel, outs, args, flops=0, scratch=()):
@@ -270,7 +273,7 @@
         in_specs=[pl.BlockSpec(memory_space=pltpu.SMEM)] + [spec] * (len(args) - 1),
         out_specs=[spec] * len(outs),
         scratch_shapes=[pltpu.VMEM(s, F32) for s in scratch],
-        compiler_params=pltpu.CompilerParams(vmem_limit_bytes=40 * 2**20),
+        compiler_params=pltpu.CompilerParams(vmem_limit_bytes=LIMIT),
         cost_estimate=pl.CostEstimate(flops=flops, bytes_accessed=moved, transcendentals=0),
     )(*args)
 
@@ -294,110 +297,85 @@
     return lax.dynamic_index_in_dim(v, i, 0, keepdims=False)
 
 
-def along(kind):
-    def move(x, d):
-        if kind == "x":
-            route = [(i, ((i // 4 + d) % 4) * 4 + i % 4) for i in range(16)]
-        else:
-            route = [(i, (i // 4) * 4 + (i + d) % 4) for i in range(16)]
-        return lax.ppermute(x, "ty", route)
-
-    return move
-
-
-def scatter_sum(v, index, n, move):
-    got = [move(at(v, (index + d) % n), d) for d in range(1, n)]
-    total = at(v, index)
-    for g in got:
-        total = total + g
-    return total
-
-
-def gather(v, index, n, move):
-    got = [v] + [move(v, d) for d in range(1, n)]
-    out = jnp.zeros((n,) + v.shape, v.dtype)
-    for d, g in enumerate(got):
-        out = lax.dynamic_update_index_in_dim(out, g, (index - d) % n, 0)
-    return out
-
-
-def sum_everywhere(grads, s):
+def exchange(x, axis, bits):
+    return lax.ppermute(x, axis, [(i, i ^ bits) for i in range(lax.axis_size(axis))])
+
+
+def scatter_sum(v, index, unit):
+    got = [exchange(at(v, index ^ d), "ty", d * unit) for d in (1, 2, 3)]
+    return at(v, index) + ((got[0] + got[1]) + got[2])
+
+
+def gather(v, index, unit):
+    got = [v] + [exchange(v, "ty", d * unit) for d in (1, 2, 3)]
+    return call(place_kernel, [(4,) + v.shape], (index[None], *got))[0]
+
+
+def after(x, *others):
+    return lax.optimization_barrier((x,) + others)[0]
+
+
+def body(object_slices, probe_modes, offsets, measured):
+    s = lax.axis_index("scan").astype(jnp.int32)
     col = lax.axis_index("ty")
     x, y = col // 4, col % 4
-    v = at(grads, s) + swap(at(grads, 1 - s))
-    v = scatter_sum(v.reshape(4, 128, W), x, 4, along("x"))
-    v = scatter_sum(v.reshape(4, 32, W), y, 4, along("y"))
-    for bit in (1, 2, 4):
-        v = v + lax.ppermute(v, "tx", [(i, i ^ bit) for i in range(8)])
-    v = gather(v, y, 4, along("y")).reshape(128, W)
-    v = gather(v, x, 4, along("x")).reshape(2, W, W)
-    other = swap(v)
-    return jnp.where(s == 0, jnp.stack([v, other]), jnp.stack([other, v]))
-
-
-def body(object_slices, probe_modes, offsets, measured):
-    s = lax.axis_index("scan").astype(jnp.int32)
     tab = jnp.asarray(tables())
     perm = jnp.asarray(deinterleave())
-
-    halos = []
-    for layer in range(2):
-        plane = at(object_slices[layer], s)
-        mine = (
-            shift(plane[:W, :], -1, 0),
-            shift(plane[:, :W], 0, -1),
-            shift(plane[:W, :W], -1, -1),
-        )
-        halos.append(mine + tuple(swap(h) for h in mine))
-
     off = offsets.reshape(2)
     off_other = swap(off)
     scal = jnp.concatenate([off, s[None]])
     pair = jnp.concatenate([off, off_other])
 
+    def strip(rows, cols):
+        zero = jnp.int32(0)
+        cut = lax.dynamic_slice(object_slices, (zero, s, zero, zero), (2, 1, rows, cols))
+        return cut.reshape(2, rows, cols)
+
+    mine = [
+        shift(strip(W, 2 * W), -1, 0),
+        shift(strip(2 * W, W), 0, -1),
+        shift(strip(W, W), -1, -1),
+    ]
     own, probe, meas = call(
         prep_kernel,
         [(2, 2, W, W), (2, 2, W, W), (W, W)],
         (off, object_slices, probe_modes, measured[0], perm),
         flops=12 * W**3,
     )
-    obj0, back = call(
-        first_kernel,
-        [(2, W, W), (2, 2, W, W)],
-        (scal, own[0], *halos[0], probe, tab),
-        flops=48 * W**3,
-    )
-    grad1, wave = call(
-        middle_kernel,
-        [(2, W, W), (2, 2, W, W)],
-        (scal, own[1], *halos[1], back, meas, tab),
-        flops=96 * W**3,
-        scratch=[(2, W, W), (2, 2, W, W)],
-    )
-    grad0, grad_probe = call(
-        last_kernel,
-        [(2, W, W), (2, 2, W, W)],
-        (scal, wave, obj0, probe, tab),
-        flops=48 * W**3,
-    )
-
-    def out(grad):
-        own_sum, below, right, diag = call(
-            spread_kernel,
-            [(2 * W, 2 * W), (W, 2 * W), (2 * W, W), (W, W)],
-            (pair, at(grad, s), swap(at(grad, 1 - s))),
-        )
-        mine = (shift(below, 1, 0), shift(right, 0, 1), shift(diag, 1, 1))
-        other = tuple(swap(h) for h in mine)
-        return call(
-            finish_kernel,
-            [(2, 2 * W, 2 * W)],
-            (s[None], own_sum, *mine, swap(own_sum), *other),
-        )[0]
-
-    tile1 = out(grad1)
-    tile0 = out(grad0)
-    return jnp.stack([tile0, tile1]), sum_everywhere(grad_probe, s)
+    mine = [after(h, own) for h in mine]
+    keep, send, probe_keep, probe_send = call(
+        gradient_kernel,
+        [(2, W, W), (2, W, W), (2, W, W), (2, W, W)],
+        (scal, own, *mine, *[swap(h) for h in mine], probe, meas, tab),
+        flops=192 * W**3,
+        scratch=[(2, 2, W, W)] * 4,
+    )
+    own_sum, below, right0, right1, diag = call(
+        spread_kernel,
+        [(2, 2 * W, 2 * W), (2, W, 2 * W), (2 * W, W), (2 * W, W), (2, W, W)],
+        (pair, keep, swap(send)),
+    )
+
+    v = probe_keep + swap(probe_send)
+    below = shift(below, 1, 0)
+    right1 = shift(right1, 0, 1)
+    v = scatter_sum(v.reshape(4, W // 2, W), x, 4)
+    v = after(v, right1)
+    v = scatter_sum(v.reshape(4, W // 8, W), y, 1)
+    v = after(v, below, right1)
+    right0 = shift(after(right0, v), 0, 1)
+    for bit in (1, 2, 4):
+        v = v + exchange(v, "tx", bit)
+    v = after(v, right0)
+    v = gather(v, y, 1).reshape(W // 2, W)
+    diag = shift(after(diag, v), 1, 1)
+    v = gather(v, x, 4).reshape(2, W, W)
+    grad_probe = call(place_kernel, [(2, 2, W, W)], (s[None], v, swap(v)))[0]
+    mine = (own_sum, below, right0, right1, diag)
+    tile = call(
+        finish_kernel, [(2, 2, 2 * W, 2 * W)], (s[None], *mine, *[swap(t) for t in mine])
+    )[0]
+    return tile, grad_probe
 
 
 def solution(mesh):

time: 193 us -> 160 us (0.83)
  the two profiles are of different devices: /device:TPU:7 before, /device:TPU:57 now
where the time goes in v2:
time: 160 us; the launch traced here: 159 us
  waiting for transfers between devices  75.1 us (47%)
  starting transfers between devices  55.8 us (35%)
  Pallas kernels  17.3 us (11%)
  local copies, waits for them, and re-layouts  7.83 us (5%)
  other arithmetic  2.51 us (2%)
    ppermute x7, waiting for transfers between devices, shift(): return lax.ppermute(x, ('tx', 'ty'), route)  43.7 us
    ppermute x15, waiting for transfers between devices, exchange(): lax.ppermute(x, axis, [(i, i ^ bits) for i in range(lax.axis_size(axis))])  25.1 us
    ppermute x15, starting transfers between devices, exchange(): lax.ppermute(x, axis, [(i, i ^ bits) for i in range(lax.axis_size(axis))])  23.6 us
    pallas_call x7, Pallas kernels, call(): pl.pallas_call(kernel, out_shape=[jax.ShapeDtypeStruct(o, F32) for o in o...  17.3 us
    ppermute x12, starting transfers between devices, swap(): return lax.ppermute(x, 'scan', [(0, 1), (1, 0)])  16.5 us
    ppermute x7, starting transfers between devices, shift(): return lax.ppermute(x, ('tx', 'ty'), route)  15.6 us
    ppermute x12, waiting for transfers between devices, swap(): return lax.ppermute(x, 'scan', [(0, 1), (1, 0)])  6.22 us
    unnamed x20, local copies, waits for them, and re-layouts  4.3 us
  transfers between devices with their start and end apart: 34, of which 17 were waited for; matrix products, arithmetic and copies ran while one was open for 3% of the time, Pallas kernels for 3%

profile of v2, /device:TPU:57, one launch (start us, length us, event | category | flops | bytes accessed | tf_op | source)
XLA Modules:
  0.0 159.4 jit_solution(442084297952038566)
XLA Ops:
  2.1 2.1 %collective-permute-start.1 = (f32[2,256,512]{2,1,0:T(8,128)S(1)}, f32[2,256,512]{2,1,0:T(8,128)S(1)}, u32[]{:S(2)}, u32[]{:S(2)}) collective-permute-start(f32[2,256,512]{2,1,0:T(8,128)S(1)} %dynamic-slice_bitcast_fusion.1), channel_id=1, source_target_pairs={{32,0},{34,2},{36,4},{38,6},{40,8},{42,10},{44,12},{46,14},{48,16}... | collective-permute-start | bytes 3145736 | tf_op jit(solution)/shard_map/ppermute | solution.py:293
  5.5 2.4 %collective-permute-start.2 = (f32[2,512,256]{2,1,0:T(8,128)S(1)}, f32[2,512,256]{2,1,0:T(8,128)S(1)}, u32[]{:S(2)}, u32[]{:S(2)}) collective-permute-start(f32[2,512,256]{2,1,0:T(8,128)S(1)} %dynamic-slice_bitcast_fusion), channel_id=1, source_target_pairs={{2,0},{4,2},{6,4},{8,6},{10,8},{12,10},{14,12},{16,14},{18,16},{20... | collective-permute-start | bytes 3145736 | tf_op jit(solution)/shard_map/ppermute | solution.py:293
  13.6 15.0 %collective-permute-done.1.b0 = f32[2,256,512]{2,1,0:T(8,128)S(1)} collective-permute-done((f32[2,256,512]{2,1,0:T(8,128)S(1)}, f32[2,256,512]{2,1,0:T(8,128)S(1)}, u32[]{:S(2)}, u32[]{:S(2)}) %collective-permute-start.1) | collective-permute-done | bytes 1048608 | tf_op jit(solution)/shard_map/ppermute | solution.py:293
  28.6 16.1 %collective-permute-done.2.r0 = f32[2,512,256]{2,1,0:T(8,128)S(1)} collective-permute-done((f32[2,512,256]{2,1,0:T(8,128)S(1)}, f32[2,512,256]{2,1,0:T(8,128)S(1)}, u32[]{:S(2)}, u32[]{:S(2)}) %collective-permute-start.2) | collective-permute-done | bytes 1048608 | tf_op jit(solution)/shard_map/ppermute | solution.py:293
  46.9 3.9 %collective-permute-done.6.d1 = f32[2,256,256]{2,1,0:T(8,128)S(1)} collective-permute-done((f32[2,256,256]{2,1,0:T(8,128)S(1)}, f32[2,256,256]{2,1,0:T(8,128)S(1)}, u32[]{:S(2)}, u32[]{:S(2)}) %collective-permute-start.6) | collective-permute-done | bytes 524320 | tf_op jit(solution)/shard_map/ppermute | solution.py:282
  50.9 7.5 %shard_map.78 = (f32[2,256,256]{2,1,0:T(8,128)S(1)}, f32[2,256,256]{2,1,0:T(8,128)S(1)}, f32[2,256,256]{2,1,0:T(8,128)S(1)}, f32[2,256,256]{2,1,0:T(8,128)}) custom-call(s32[3]{0:T(128)S(1)} %pad_add_fusion.1.scal, f32[2,2,256,256]{3,2,1,0:T(8,128)S(1)} %get-tuple-element.22.own, f32[2,256,512]{2,1,0:T(8,128)S(1)} %collective-permute-done.1.b0, ...), custom_call_target="tpu_custom_call" | custom-call | flops 3221225472 | bytes 11796492 | tf_op jit(solution)/shard_map/pallas_call | solution.py:270
  60.4 2.6 %shard_map.79 = (f32[2,512,512]{2,1,0:T(8,128)S(1)}, f32[2,256,512]{2,1,0:T(8,128)}, f32[512,256]{1,0:T(8,128)S(1)}, f32[512,256]{1,0:T(8,128)}, f32[2,256,256]{2,1,0:T(8,128)S(1)}) custom-call(s32[4]{0:T(128)S(1)} %pad_add_fusion.scal, f32[2,256,256]{2,1,0:T(8,128)S(1)} %get-tuple-element.28.mine, f32[2,256,256]{2,1,0:T(8,128)S(1)} %collective-permute-done.7.other), custom_call_target="tpu_custom_call" | custom-call | bytes 5767184 | tf_op jit(solution)/shard_map/pallas_call | solution.py:270
  64.6 3.5 %collective-permute-start.8 = (f32[2,256,512]{2,1,0:T(8,128)}, f32[2,256,512]{2,1,0:T(8,128)S(1)}, u32[]{:S(2)}, u32[]{:S(2)}) collective-permute-start(f32[2,256,512]{2,1,0:T(8,128)} %get-tuple-element.31), channel_id=1, source_target_pairs={{0,32},{2,34},{4,36},{6,38},{8,40},{10,42},{12,44},{14,46},{16,48}... | collective-permute-start | bytes 3145736 | tf_op jit(solution)/shard_map/ppermute | solution.py:293
  68.1 1.9 %collective-permute-start.13 = (f32[512,256]{1,0:T(8,128)}, f32[512,256]{1,0:T(8,128)}, u32[]{:S(2)}, u32[]{:S(2)}) collective-permute-start(f32[512,256]{1,0:T(8,128)} %get-tuple-element.35), channel_id=1, source_target_pairs={{0,2},{2,4},{4,6},{6,8},{8,10},{10,12},{12,14},{14,16},{16,18},{18... | collective-permute-start | bytes 1572872 | tf_op jit(solution)/shard_map/ppermute | solution.py:293
  72.8 2.4 %collective-permute-start.10 = (f32[128,256]{1,0:T(8,128)S(1)}, f32[128,256]{1,0:T(8,128)}, u32[]{:S(2)}, u32[]{:S(2)}) collective-permute-start(f32[128,256]{1,0:T(8,128)S(1)} %get-tuple-element.44), channel_id=1, source_target_pairs={{0,8},{2,10},{4,12},{6,14},{8,0},{10,2},{12,4},{14,6},{16,24},{18,... | collective-permute-start | bytes 393224 | tf_op jit(solution)/shard_map/ppermute | solution.py:301
  76.7 2.0 %collective-permute-done.12 = f32[128,256]{1,0:T(8,128)S(1)} collective-permute-done((f32[128,256]{1,0:T(8,128)}, f32[128,256]{1,0:T(8,128)S(1)}, u32[]{:S(2)}, u32[]{:S(2)}) %collective-permute-start.12) | collective-permute-done | bytes 131104 | tf_op jit(solution)/shard_map/ppermute | solution.py:301
  80.2 3.8 %collective-permute-done.10 = f32[128,256]{1,0:T(8,128)} collective-permute-done((f32[128,256]{1,0:T(8,128)S(1)}, f32[128,256]{1,0:T(8,128)}, u32[]{:S(2)}, u32[]{:S(2)}) %collective-permute-start.10) | collective-permute-done | bytes 131104 | tf_op jit(solution)/shard_map/ppermute | solution.py:301
  84.0 6.4 %collective-permute-done.11 = f32[128,256]{1,0:T(8,128)} collective-permute-done((f32[128,256]{1,0:T(8,128)S(1)}, f32[128,256]{1,0:T(8,128)}, u32[]{:S(2)}, u32[]{:S(2)}) %collective-permute-start.11) | collective-permute-done | bytes 131104 | tf_op jit(solution)/shard_map/ppermute | solution.py:301
  91.7 3.7 %collective-permute-start.15 = (f32[32,256]{1,0:T(8,128)S(1)}, f32[32,256]{1,0:T(8,128)S(1)}, u32[]{:S(2)}, u32[]{:S(2)}) collective-permute-start(f32[32,256]{1,0:T(8,128)S(1)} %get-tuple-element.45), channel_id=1, source_target_pairs={{0,4},{2,6},{4,0},{6,2},{8,12},{10,14},{12,8},{14,10},{16,20},{18,... | collective-permute-start | bytes 98312 | tf_op jit(solution)/shard_map/ppermute | solution.py:301
  99.1 2.8 %collective-permute-done.18 = f32[32,256]{1,0:T(8,128)S(1)} collective-permute-done((f32[32,256]{1,0:T(8,128)S(1)}, f32[32,256]{1,0:T(8,128)S(1)}, u32[]{:S(2)}, u32[]{:S(2)}) %collective-permute-start.18) | collective-permute-done | bytes 32800 | tf_op jit(solution)/shard_map/ppermute | solution.py:301
  101.9 4.2 %collective-permute-start.19 = (f32[32,256]{1,0:T(8,128)S(1)}, f32[32,256]{1,0:T(8,128)S(1)}, u32[]{:S(2)}, u32[]{:S(2)}) collective-permute-start(f32[32,256]{1,0:T(8,128)S(1)} %add.83), channel_id=1, source_target_pairs={{0,64},{32,96},{64,0},{96,32},{128,192},{160,224},{192,128},{224,1... | collective-permute-start | bytes 98312 | tf_op jit(solution)/shard_map/ppermute | solution.py:301
  107.8 3.6 %collective-permute-start.20 = (f32[32,256]{1,0:T(8,128)S(1)}, f32[32,256]{1,0:T(8,128)S(1)}, u32[]{:S(2)}, u32[]{:S(2)}) collective-permute-start(f32[32,256]{1,0:T(8,128)S(1)} %add.84), channel_id=1, source_target_pairs={{0,128},{32,160},{64,192},{96,224},{128,0},{160,32},{192,64},{224,... | collective-permute-start | bytes 98312 | tf_op jit(solution)/shard_map/ppermute | solution.py:301
  111.4 3.1 %collective-permute-done.20 = f32[32,256]{1,0:T(8,128)S(1)} collective-permute-done((f32[32,256]{1,0:T(8,128)S(1)}, f32[32,256]{1,0:T(8,128)S(1)}, u32[]{:S(2)}, u32[]{:S(2)}) %collective-permute-start.20) | collective-permute-done | bytes 32800 | tf_op jit(solution)/shard_map/ppermute | solution.py:301
  115.7 2.6 %collective-permute-start.22 = (f32[32,256]{1,0:T(8,128)S(1)}, f32[32,256]{1,0:T(8,128)S(1)}, u32[]{:S(2)}, u32[]{:S(2)}) collective-permute-start(f32[32,256]{1,0:T(8,128)S(1)} %add.85.refs_0_), channel_id=1, source_target_pairs={{0,4},{2,6},{4,0},{6,2},{8,12},{10,14},{12,8},{14,10},{16,20},{18,... | collective-permute-start | bytes 98312 | tf_op jit(solution)/shard_map/ppermute | solution.py:301
  120.0 2.3 %collective-permute-done.23.refs_3_ = f32[32,256]{1,0:T(8,128)S(1)} collective-permute-done((f32[32,256]{1,0:T(8,128)S(1)}, f32[32,256]{1,0:T(8,128)S(1)}, u32[]{:S(2)}, u32[]{:S(2)}) %collective-permute-start.23) | collective-permute-done | bytes 32800 | tf_op jit(solution)/shard_map/ppermute | solution.py:301
  123.0 3.2 %collective-permute-start.32 = (f32[128,256]{1,0:T(8,128)S(1)}, f32[128,256]{1,0:T(8,128)S(1)}, u32[]{:S(2)}, u32[]{:S(2)}) collective-permute-start(f32[128,256]{1,0:T(8,128)S(1)} %bitcast.35), channel_id=1, source_target_pairs={{0,24},{2,26},{4,28},{6,30},{8,16},{10,18},{12,20},{14,22},{16,8},... | collective-permute-start | bytes 393224 | tf_op jit(solution)/shard_map/ppermute | solution.py:301
  126.2 9.3 %collective-permute-start.26 = (f32[2,256,512]{2,1,0:T(8,128)S(1)}, f32[2,256,512]{2,1,0:T(8,128)S(1)}, u32[]{:S(2)}, u32[]{:S(2)}) collective-permute-start(f32[2,256,512]{2,1,0:T(8,128)S(1)} %collective-permute-done.8.b0), channel_id=1, source_target_pairs={{0,1},{1,0},{2,3},{3,2},{4,5},{5,4},{6,7},{7,6},{8,9},{9,8},{10,11... | collective-permute-start | bytes 3145736 | tf_op jit(solution)/shard_map/ppermute | solution.py:282
  139.1 12.7 %collective-permute-done.24.d0 = f32[2,256,256]{2,1,0:T(8,128)S(1)} collective-permute-done((f32[2,256,256]{2,1,0:T(8,128)}, f32[2,256,256]{2,1,0:T(8,128)S(1)}, u32[]{:S(2)}, u32[]{:S(2)}) %collective-permute-start.24) | collective-permute-done | bytes 524320 | tf_op jit(solution)/shard_map/ppermute | solution.py:293
  155.1 4.3 %shard_map.81 = f32[2,2,512,512]{3,2,1,0:T(8,128)} custom-call(s32[1]{0:T(128)} %bitcast.scal, f32[2,512,512]{2,1,0:T(8,128)S(1)} %get-tuple-element.30.own0, f32[2,256,512]{2,1,0:T(8,128)S(1)} %collective-permute-done.8.b0, f32[512,256]{1,0:T(8,128)S(1)} %collective-permute-done.17.r00, f32[512,256]{1,0:T(8,128)} %collective-permute-done.13.r01, ...), custom_call_target="tpu_custom_call" | custom-call | bytes 13631492 | tf_op jit(solution)/shard_map/pallas_call | solution.py:270
  (84 shorter events, 37.2 us)
Async XLA Ops:
  2.1 26.4 %collective-permute-start.1 = (f32[2,256,512]{2,1,0:T(8,128)S(1)}, f32[2,256,512]{2,1,0:T(8,128)S(1)}, u32[]{:S(2)}, u32[]{:S(2)}) collective-permute-start(f32[2,256,512]{2,1,0:T(8,128)S(1)} %dynamic-slice_bitcast_fusion.1), channel_id=1, source_target_pairs={{32,0},{34,2},{36,4},{38,6},{40,8},{42,10},{44,12},{46,14},{48,16}... | collective-permute-start | bytes 3145736 | tf_op jit(solution)/shard_map/ppermute | solution.py:293
  5.5 39.2 %collective-permute-start.2 = (f32[2,512,256]{2,1,0:T(8,128)S(1)}, f32[2,512,256]{2,1,0:T(8,128)S(1)}, u32[]{:S(2)}, u32[]{:S(2)}) collective-permute-start(f32[2,512,256]{2,1,0:T(8,128)S(1)} %dynamic-slice_bitcast_fusion), channel_id=1, source_target_pairs={{2,0},{4,2},{6,4},{8,6},{10,8},{12,10},{14,12},{16,14},{18,16},{20... | collective-permute-start | bytes 3145736 | tf_op jit(solution)/shard_map/ppermute | solution.py:293
  7.9 38.4 %collective-permute-start.3 = (f32[2,256,256]{2,1,0:T(8,128)S(1)}, f32[2,256,256]{2,1,0:T(8,128)S(1)}, u32[]{:S(2)}, u32[]{:S(2)}) collective-permute-start(f32[2,256,256]{2,1,0:T(8,128)S(1)} %dynamic-slice_bitcast_fusion.2), channel_id=1, source_target_pairs={{34,0},{36,2},{38,4},{40,6},{42,8},{44,10},{46,12},{48,14},{50,16}... | collective-permute-start | bytes 1572872 | tf_op jit(solution)/shard_map/ppermute | solution.py:293
  44.7 6.2 %collective-permute-start.4 = (f32[2,256,512]{2,1,0:T(8,128)S(1)}, f32[2,256,512]{2,1,0:T(8,128)S(1)}, u32[]{:S(2)}, u32[]{:S(2)}) collective-permute-start(f32[2,256,512]{2,1,0:T(8,128)S(1)} %collective-permute-done.1.b0), channel_id=1, source_target_pairs={{0,1},{1,0},{2,3},{3,2},{4,5},{5,4},{6,7},{7,6},{8,9},{9,8},{10,11... | collective-permute-start | bytes 3145736 | tf_op jit(solution)/shard_map/ppermute | solution.py:282
  46.3 4.5 %collective-permute-start.5 = (f32[2,512,256]{2,1,0:T(8,128)S(1)}, f32[2,512,256]{2,1,0:T(8,128)S(1)}, u32[]{:S(2)}, u32[]{:S(2)}) collective-permute-start(f32[2,512,256]{2,1,0:T(8,128)S(1)} %collective-permute-done.2.r0), channel_id=1, source_target_pairs={{0,1},{1,0},{2,3},{3,2},{4,5},{5,4},{6,7},{7,6},{8,9},{9,8},{10,11... | collective-permute-start | bytes 3145736 | tf_op jit(solution)/shard_map/ppermute | solution.py:282
  46.3 4.5 %collective-permute-start.6 = (f32[2,256,256]{2,1,0:T(8,128)S(1)}, f32[2,256,256]{2,1,0:T(8,128)S(1)}, u32[]{:S(2)}, u32[]{:S(2)}) collective-permute-start(f32[2,256,256]{2,1,0:T(8,128)S(1)} %collective-permute-done.3.d0), channel_id=1, source_target_pairs={{0,1},{1,0},{2,3},{3,2},{4,5},{5,4},{6,7},{7,6},{8,9},{9,8},{10,11... | collective-permute-start | bytes 1572872 | tf_op jit(solution)/shard_map/ppermute | solution.py:282
  58.8 11.3 %collective-permute-start.9 = (f32[2,256,256]{2,1,0:T(8,128)}, f32[2,256,256]{2,1,0:T(8,128)}, u32[]{:S(2)}, u32[]{:S(2)}) collective-permute-start(f32[2,256,256]{2,1,0:T(8,128)} %get-tuple-element.34), channel_id=1, source_target_pairs={{0,1},{1,0},{2,3},{3,2},{4,5},{5,4},{6,7},{7,6},{8,9},{9,8},{10,11... | collective-permute-start | bytes 1572872 | tf_op jit(solution)/shard_map/ppermute | solution.py:282
  64.6 32.5 %collective-permute-start.8 = (f32[2,256,512]{2,1,0:T(8,128)}, f32[2,256,512]{2,1,0:T(8,128)S(1)}, u32[]{:S(2)}, u32[]{:S(2)}) collective-permute-start(f32[2,256,512]{2,1,0:T(8,128)} %get-tuple-element.31), channel_id=1, source_target_pairs={{0,32},{2,34},{4,36},{6,38},{8,40},{10,42},{12,44},{14,46},{16,48}... | collective-permute-start | bytes 3145736 | tf_op jit(solution)/shard_map/ppermute | solution.py:293
  68.1 23.3 %collective-permute-start.13 = (f32[512,256]{1,0:T(8,128)}, f32[512,256]{1,0:T(8,128)}, u32[]{:S(2)}, u32[]{:S(2)}) collective-permute-start(f32[512,256]{1,0:T(8,128)} %get-tuple-element.35), channel_id=1, source_target_pairs={{0,2},{2,4},{4,6},{6,8},{8,10},{10,12},{12,14},{14,16},{16,18},{18... | collective-permute-start | bytes 1572872 | tf_op jit(solution)/shard_map/ppermute | solution.py:293
  72.8 5.8 %collective-permute-start.12 = (f32[128,256]{1,0:T(8,128)}, f32[128,256]{1,0:T(8,128)S(1)}, u32[]{:S(2)}, u32[]{:S(2)}) collective-permute-start(f32[128,256]{1,0:T(8,128)} %get-tuple-element.43), channel_id=1, source_target_pairs={{0,24},{2,26},{4,28},{6,30},{8,16},{10,18},{12,20},{14,22},{16,8},... | collective-permute-start | bytes 393224 | tf_op jit(solution)/shard_map/ppermute | solution.py:301
  72.8 11.1 %collective-permute-start.10 = (f32[128,256]{1,0:T(8,128)S(1)}, f32[128,256]{1,0:T(8,128)}, u32[]{:S(2)}, u32[]{:S(2)}) collective-permute-start(f32[128,256]{1,0:T(8,128)S(1)} %get-tuple-element.44), channel_id=1, source_target_pairs={{0,8},{2,10},{4,12},{6,14},{8,0},{10,2},{12,4},{14,6},{16,24},{18,... | collective-permute-start | bytes 393224 | tf_op jit(solution)/shard_map/ppermute | solution.py:301
  75.3 15.1 %collective-permute-start.11 = (f32[128,256]{1,0:T(8,128)S(1)}, f32[128,256]{1,0:T(8,128)}, u32[]{:S(2)}, u32[]{:S(2)}) collective-permute-start(f32[128,256]{1,0:T(8,128)S(1)} %get-tuple-element.42), channel_id=1, source_target_pairs={{0,16},{2,18},{4,20},{6,22},{8,24},{10,26},{12,28},{14,30},{16,0},... | collective-permute-start | bytes 393224 | tf_op jit(solution)/shard_map/ppermute | solution.py:301
  78.6 75.2 %collective-permute-start.25 = (f32[2,512,512]{2,1,0:T(8,128)S(1)}, f32[2,512,512]{2,1,0:T(8,128)}, u32[]{:S(2)}, u32[]{:S(2)}) collective-permute-start(f32[2,512,512]{2,1,0:T(8,128)S(1)} %get-tuple-element.30.own0), channel_id=1, source_target_pairs={{0,1},{1,0},{2,3},{3,2},{4,5},{5,4},{6,7},{7,6},{8,9},{9,8},{10,11... | collective-permute-start | bytes 6291464 | tf_op jit(solution)/shard_map/ppermute | solution.py:282
  91.7 5.4 %collective-permute-start.15 = (f32[32,256]{1,0:T(8,128)S(1)}, f32[32,256]{1,0:T(8,128)S(1)}, u32[]{:S(2)}, u32[]{:S(2)}) collective-permute-start(f32[32,256]{1,0:T(8,128)S(1)} %get-tuple-element.45), channel_id=1, source_target_pairs={{0,4},{2,6},{4,0},{6,2},{8,12},{10,14},{12,8},{14,10},{16,20},{18,... | collective-permute-start | bytes 98312 | tf_op jit(solution)/shard_map/ppermute | solution.py:301
  97.1 17.3 %collective-permute-start.17 = (f32[512,256]{1,0:T(8,128)}, f32[512,256]{1,0:T(8,128)S(1)}, u32[]{:S(2)}, u32[]{:S(2)}) collective-permute-start(f32[512,256]{1,0:T(8,128)} %copy-done.7), channel_id=1, source_target_pairs={{0,2},{2,4},{4,6},{6,8},{8,10},{10,12},{12,14},{14,16},{16,18},{18... | collective-permute-start | bytes 1572872 | tf_op jit(solution)/shard_map/ppermute | solution.py:293
  101.9 5.9 %collective-permute-start.19 = (f32[32,256]{1,0:T(8,128)S(1)}, f32[32,256]{1,0:T(8,128)S(1)}, u32[]{:S(2)}, u32[]{:S(2)}) collective-permute-start(f32[32,256]{1,0:T(8,128)S(1)} %add.83), channel_id=1, source_target_pairs={{0,64},{32,96},{64,0},{96,32},{128,192},{160,224},{192,128},{224,1... | collective-permute-start | bytes 98312 | tf_op jit(solution)/shard_map/ppermute | solution.py:301
  107.8 6.7 %collective-permute-start.20 = (f32[32,256]{1,0:T(8,128)S(1)}, f32[32,256]{1,0:T(8,128)S(1)}, u32[]{:S(2)}, u32[]{:S(2)}) collective-permute-start(f32[32,256]{1,0:T(8,128)S(1)} %add.84), channel_id=1, source_target_pairs={{0,128},{32,160},{64,192},{96,224},{128,0},{160,32},{192,64},{224,... | collective-permute-start | bytes 98312 | tf_op jit(solution)/shard_map/ppermute | solution.py:301
  122.3 13.2 %collective-permute-start.30 = (f32[128,256]{1,0:T(8,128)S(1)}, f32[128,256]{1,0:T(8,128)S(1)}, u32[]{:S(2)}, u32[]{:S(2)}) collective-permute-start(f32[128,256]{1,0:T(8,128)S(1)} %bitcast.33), channel_id=1, source_target_pairs={{0,8},{2,10},{4,12},{6,14},{8,0},{10,2},{12,4},{14,6},{16,24},{18,... | collective-permute-start | bytes 393224 | tf_op jit(solution)/shard_map/ppermute | solution.py:301
  122.4 15.0 %collective-permute-start.31 = (f32[128,256]{1,0:T(8,128)S(1)}, f32[128,256]{1,0:T(8,128)S(1)}, u32[]{:S(2)}, u32[]{:S(2)}) collective-permute-start(f32[128,256]{1,0:T(8,128)S(1)} %bitcast.34), channel_id=1, source_target_pairs={{0,16},{2,18},{4,20},{6,22},{8,24},{10,26},{12,28},{14,30},{16,0},... | collective-permute-start | bytes 393224 | tf_op jit(solution)/shard_map/ppermute | solution.py:301
  123.0 14.4 %collective-permute-start.32 = (f32[128,256]{1,0:T(8,128)S(1)}, f32[128,256]{1,0:T(8,128)S(1)}, u32[]{:S(2)}, u32[]{:S(2)}) collective-permute-start(f32[128,256]{1,0:T(8,128)S(1)} %bitcast.35), channel_id=1, source_target_pairs={{0,24},{2,26},{4,28},{6,30},{8,16},{10,18},{12,20},{14,22},{16,8},... | collective-permute-start | bytes 393224 | tf_op jit(solution)/shard_map/ppermute | solution.py:301
  126.2 28.1 %collective-permute-start.26 = (f32[2,256,512]{2,1,0:T(8,128)S(1)}, f32[2,256,512]{2,1,0:T(8,128)S(1)}, u32[]{:S(2)}, u32[]{:S(2)}) collective-permute-start(f32[2,256,512]{2,1,0:T(8,128)S(1)} %collective-permute-done.8.b0), channel_id=1, source_target_pairs={{0,1},{1,0},{2,3},{3,2},{4,5},{5,4},{6,7},{7,6},{8,9},{9,8},{10,11... | collective-permute-start | bytes 3145736 | tf_op jit(solution)/shard_map/ppermute | solution.py:282
  135.5 16.2 %collective-permute-start.24 = (f32[2,256,256]{2,1,0:T(8,128)}, f32[2,256,256]{2,1,0:T(8,128)S(1)}, u32[]{:S(2)}, u32[]{:S(2)}) collective-permute-start(f32[2,256,256]{2,1,0:T(8,128)} %copy-done.6), channel_id=1, source_target_pairs={{0,34},{2,36},{4,38},{6,40},{8,42},{10,44},{12,46},{14,48},{16,50}... | collective-permute-start | bytes 1572872 | tf_op jit(solution)/shard_map/ppermute | solution.py:293
  137.5 15.3 %collective-permute-start.33 = (f32[2,256,256]{2,1,0:T(8,128)S(1)}, f32[2,256,256]{2,1,0:T(8,128)S(1)}, u32[]{:S(2)}, u32[]{:S(2)}) collective-permute-start(f32[2,256,256]{2,1,0:T(8,128)S(1)} %bitcast.31), channel_id=1, source_target_pairs={{0,1},{1,0},{2,3},{3,2},{4,5},{5,4},{6,7},{7,6},{8,9},{9,8},{10,11... | collective-permute-start | bytes 1572872 | tf_op jit(solution)/shard_map/ppermute | solution.py:282
  139.0 14.9 %collective-permute-start.28 = (f32[512,256]{1,0:T(8,128)}, f32[512,256]{1,0:T(8,128)S(1)}, u32[]{:S(2)}, u32[]{:S(2)}) collective-permute-start(f32[512,256]{1,0:T(8,128)} %collective-permute-done.13.r01), channel_id=1, source_target_pairs={{0,1},{1,0},{2,3},{3,2},{4,5},{5,4},{6,7},{7,6},{8,9},{9,8},{10,11... | collective-permute-start | bytes 1572872 | tf_op jit(solution)/shard_map/ppermute | solution.py:282
  (20 other events, 105.1 us)

commit v3 on v2

--- a/solution.py
+++ b/solution.py
@@ -243,16 +243,38 @@
                     diag_out[k] = v
 
 
-def finish_kernel(scal, own0, b0, r00, r01, d0, own1, b1, r10, r11, d1, out):
+def finish_kernel(scal, own0, b0, r00, r01, own1, b1, r10, r11, out, part):
     s = scal[0]
     for k in range(2):
-        mine = (own0, b0, (r00, r01)[k], d0)
-        other = (own1, b1, (r10, r11)[k], d1)
-        for plane, (own, b, r, d) in ((s, mine), (1 - s, other)):
+        mine = (own0, b0, (r00, r01)[k])
+        other = (own1, b1, (r10, r11)[k])
+        for plane, (own, b, r) in ((s, mine), (1 - s, other)):
             out[k, plane, W:, W:] = own[k, W:, W:]
-            out[k, plane, :W, :W] = own[k, :W, :W] + (b[k, :, :W] + r[:W, :] + d[k])
+            part[k, plane] = own[k, :W, :W] + (b[k, :, :W] + r[:W, :])
             out[k, plane, :W, W:] = own[k, :W, W:] + b[k, :, W:]
             out[k, plane, W:, :W] = own[k, W:, :W] + r[W:, :]
+
+
+def corner_kernel(scal, mine, other, part, tile, out):
+    s = scal[0]
+    for k in range(2):
+        out[k, s] = part[k, s] + mine[k]
+        out[k, 1 - s] = part[k, 1 - s] + other[k]
+
+
+def add_corner(s, mine, other, part, tile):
+    spec = pl.BlockSpec(memory_space=pltpu.VMEM)
+    return pl.pallas_call(
+        corner_kernel,
+        grid=(1,),
+        out_shape=jax.ShapeDtypeStruct(tile.shape, F32),
+        in_specs=[pl.BlockSpec(memory_space=pltpu.SMEM), spec, spec, spec]
+        + [pl.BlockSpec(memory_space=pl.ANY)],
+        out_specs=pl.BlockSpec((2, 2, W, W), lambda i: (0, 0, 0, 0)),
+        input_output_aliases={4: 0},
+        compiler_params=pltpu.CompilerParams(vmem_limit_bytes=LIMIT),
+        cost_estimate=pl.CostEstimate(flops=0, bytes_accessed=2**21, transcendentals=0),
+    )(s[None], mine, other, part, tile)
 
 
 def place_kernel(scal, *refs):
@@ -363,19 +385,22 @@
     v = after(v, right1)
     v = scatter_sum(v.reshape(4, W // 8, W), y, 1)
     v = after(v, below, right1)
+    others = [swap(t) for t in (own_sum, below, right1)]
     right0 = shift(after(right0, v), 0, 1)
     for bit in (1, 2, 4):
         v = v + exchange(v, "tx", bit)
-    v = after(v, right0)
+    v = after(v, right0, *others)
     v = gather(v, y, 1).reshape(W // 2, W)
     diag = shift(after(diag, v), 1, 1)
-    v = gather(v, x, 4).reshape(2, W, W)
+    own_o, below_o, right1_o = others
+    tile, part = call(
+        finish_kernel,
+        [(2, 2, 2 * W, 2 * W), (2, 2, W, W)],
+        (s[None], own_sum, below, right0, right1, own_o, below_o, swap(right0), right1_o),
+    )
+    v = after(gather(v, x, 4), part).reshape(2, W, W)
     grad_probe = call(place_kernel, [(2, 2, W, W)], (s[None], v, swap(v)))[0]
-    mine = (own_sum, below, right0, right1, diag)
-    tile = call(
-        finish_kernel, [(2, 2, 2 * W, 2 * W)], (s[None], *mine, *[swap(t) for t in mine])
-    )[0]
-    return tile, grad_probe
+    return add_corner(s, diag, swap(diag), part, tile), grad_probe
 
 
 def solution(mesh):

time: 160 us -> 156 us (0.975)
  waiting for transfers between devices: 75.1 us -> 65.2 us
  starting transfers between devices: 55.8 us -> 60.1 us
    ppermute x7, waiting for transfers between devices: 43.7 us -> 30.9 us  [shift(): return lax.ppermute(x, ('tx', 'ty'), route)]
    ppermute x12, waiting for transfers between devices: 6.22 us -> 8.53 us  [swap(): return lax.ppermute(x, 'scan', [(0, 1), (1, 0)])]
    ppermute x7, starting transfers between devices: 15.6 us -> 17.6 us  [shift(): return lax.ppermute(x, ('tx', 'ty'), route)]
    unnamed x20 -> x22, local copies, waits for them, and re-layouts: 4.3 us -> 5.11 us
  transfers between devices with their start and end apart: 34 -> 34, of which waited for: 17 -> 14; matrix products, arithmetic and copies ran while one was open for 3% -> 3% of each run, Pallas kernels for 3% -> 5%
where the time goes in v3:
time: 156 us; the launch traced here: 155 us
  waiting for transfers between devices  65.2 us (42%)
  starting transfers between devices  60.1 us (39%)
  Pallas kernels  18.5 us (12%)
  local copies, waits for them, and re-layouts  7.97 us (5%)
  other arithmetic  2.51 us (2%)
    ppermute x7, waiting for transfers between devices, shift(): return lax.ppermute(x, ('tx', 'ty'), route)  30.9 us
    ppermute x15, waiting for transfers between devices, exchange(): lax.ppermute(x, axis, [(i, i ^ bits) for i in range(lax.axis_size(axis))])  25.8 us
    ppermute x15, starting transfers between devices, exchange(): lax.ppermute(x, axis, [(i, i ^ bits) for i in range(lax.axis_size(axis))])  24.8 us
    ppermute x12, starting transfers between devices, swap(): return lax.ppermute(x, 'scan', [(0, 1), (1, 0)])  17.7 us
    ppermute x7, starting transfers between devices, shift(): return lax.ppermute(x, ('tx', 'ty'), route)  17.6 us
    pallas_call x7, Pallas kernels, call(): pl.pallas_call(kernel, out_shape=[jax.ShapeDtypeStruct(o, F32) for o in o...  17.4 us
    ppermute x12, waiting for transfers between devices, swap(): return lax.ppermute(x, 'scan', [(0, 1), (1, 0)])  8.53 us
    unnamed x22, local copies, waits for them, and re-layouts  5.11 us
  transfers between devices with their start and end apart: 34, of which 14 were waited for; matrix products, arithmetic and copies ran while one was open for 3% of the time, Pallas kernels for 5%

profile of v3, /device:TPU:57, one launch (start us, length us, event | category | flops | bytes accessed | tf_op | source)
XLA Modules:
  0.0 155.2 jit_solution(17840075147328749807)
XLA Ops:
  5.5 2.4 %collective-permute-start.2 = (f32[2,512,256]{2,1,0:T(8,128)S(1)}, f32[2,512,256]{2,1,0:T(8,128)S(1)}, u32[]{:S(2)}, u32[]{:S(2)}) collective-permute-start(f32[2,512,256]{2,1,0:T(8,128)S(1)} %dynamic-slice_bitcast_fusion), channel_id=1, source_target_pairs={{2,0},{4,2},{6,4},{8,6},{10,8},{12,10},{14,12},{16,14},{18,16},{20... | collective-permute-start | bytes 3145736 | tf_op jit(solution)/shard_map/ppermute | solution.py:315
  13.6 15.0 %collective-permute-done.1.b0 = f32[2,256,512]{2,1,0:T(8,128)S(1)} collective-permute-done((f32[2,256,512]{2,1,0:T(8,128)S(1)}, f32[2,256,512]{2,1,0:T(8,128)S(1)}, u32[]{:S(2)}, u32[]{:S(2)}) %collective-permute-start.1) | collective-permute-done | bytes 1048608 | tf_op jit(solution)/shard_map/ppermute | solution.py:315
  28.6 2.3 %collective-permute-start.4 = (f32[2,256,512]{2,1,0:T(8,128)S(1)}, f32[2,256,512]{2,1,0:T(8,128)S(1)}, u32[]{:S(2)}, u32[]{:S(2)}) collective-permute-start(f32[2,256,512]{2,1,0:T(8,128)S(1)} %collective-permute-done.1.b0), channel_id=1, source_target_pairs={{0,1},{1,0},{2,3},{3,2},{4,5},{5,4},{6,7},{7,6},{8,9},{9,8},{10,11... | collective-permute-start | bytes 3145736 | tf_op jit(solution)/shard_map/ppermute | solution.py:304
  30.8 13.8 %collective-permute-done.2.r0 = f32[2,512,256]{2,1,0:T(8,128)S(1)} collective-permute-done((f32[2,512,256]{2,1,0:T(8,128)S(1)}, f32[2,512,256]{2,1,0:T(8,128)S(1)}, u32[]{:S(2)}, u32[]{:S(2)}) %collective-permute-start.2) | collective-permute-done | bytes 1048608 | tf_op jit(solution)/shard_map/ppermute | solution.py:315
  46.4 3.0 %collective-permute-done.6.d1 = f32[2,256,256]{2,1,0:T(8,128)S(1)} collective-permute-done((f32[2,256,256]{2,1,0:T(8,128)S(1)}, f32[2,256,256]{2,1,0:T(8,128)S(1)}, u32[]{:S(2)}, u32[]{:S(2)}) %collective-permute-start.6) | collective-permute-done | bytes 524320 | tf_op jit(solution)/shard_map/ppermute | solution.py:304
  49.4 7.4 %shard_map.78 = (f32[2,256,256]{2,1,0:T(8,128)S(1)}, f32[2,256,256]{2,1,0:T(8,128)S(1)}, f32[2,256,256]{2,1,0:T(8,128)S(1)}, f32[2,256,256]{2,1,0:T(8,128)}) custom-call(s32[3]{0:T(128)S(1)} %pad_add_fusion.1.scal, f32[2,2,256,256]{3,2,1,0:T(8,128)S(1)} %get-tuple-element.25.own, f32[2,256,512]{2,1,0:T(8,128)S(1)} %collective-permute-done.1.b0, ...), custom_call_target="tpu_custom_call" | custom-call | flops 3221225472 | bytes 11796492 | tf_op jit(solution)/shard_map/pallas_call | solution.py:292
  58.8 2.7 %shard_map.79 = (f32[2,512,512]{2,1,0:T(8,128)S(1)}, f32[2,256,512]{2,1,0:T(8,128)}, f32[512,256]{1,0:T(8,128)S(1)}, f32[512,256]{1,0:T(8,128)S(1)}, f32[2,256,256]{2,1,0:T(8,128)S(1)}) custom-call(s32[4]{0:T(128)S(1)} %pad_add_fusion.scal, f32[2,256,256]{2,1,0:T(8,128)S(1)} %get-tuple-element.31.mine, f32[2,256,256]{2,1,0:T(8,128)S(1)} %collective-permute-done.7.other), custom_call_target="tpu_custom_call" | custom-call | bytes 5767184 | tf_op jit(solution)/shard_map/pallas_call | solution.py:292
  63.9 3.5 %collective-permute-start.16 = (f32[2,256,512]{2,1,0:T(8,128)}, f32[2,256,512]{2,1,0:T(8,128)S(1)}, u32[]{:S(2)}, u32[]{:S(2)}) collective-permute-start(f32[2,256,512]{2,1,0:T(8,128)} %get-tuple-element.38), channel_id=1, source_target_pairs={{0,32},{2,34},{4,36},{6,38},{8,40},{10,42},{12,44},{14,46},{16,48}... | collective-permute-start | bytes 3145736 | tf_op jit(solution)/shard_map/ppermute | solution.py:315
  70.3 2.7 %collective-permute-done.8 = f32[2,256,256]{2,1,0:T(8,128)} collective-permute-done((f32[2,256,256]{2,1,0:T(8,128)}, f32[2,256,256]{2,1,0:T(8,128)}, u32[]{:S(2)}, u32[]{:S(2)}) %collective-permute-start.8) | collective-permute-done | bytes 524320 | tf_op jit(solution)/shard_map/ppermute | solution.py:304
  75.1 2.9 %collective-permute-start.10 = (f32[128,256]{1,0:T(8,128)S(1)}, f32[128,256]{1,0:T(8,128)S(1)}, u32[]{:S(2)}, u32[]{:S(2)}) collective-permute-start(f32[128,256]{1,0:T(8,128)S(1)} %get-tuple-element.48), channel_id=1, source_target_pairs={{0,16},{2,18},{4,20},{6,22},{8,24},{10,26},{12,28},{14,30},{16,0},... | collective-permute-start | bytes 393224 | tf_op jit(solution)/shard_map/ppermute | solution.py:323
  78.8 9.5 %collective-permute-done.10 = f32[128,256]{1,0:T(8,128)S(1)} collective-permute-done((f32[128,256]{1,0:T(8,128)S(1)}, f32[128,256]{1,0:T(8,128)S(1)}, u32[]{:S(2)}, u32[]{:S(2)}) %collective-permute-start.10) | collective-permute-done | bytes 131104 | tf_op jit(solution)/shard_map/ppermute | solution.py:323
  94.0 3.7 %collective-permute-start.15 = (f32[32,256]{1,0:T(8,128)S(1)}, f32[32,256]{1,0:T(8,128)S(1)}, u32[]{:S(2)}, u32[]{:S(2)}) collective-permute-start(f32[32,256]{1,0:T(8,128)S(1)} %get-tuple-element.52), channel_id=1, source_target_pairs={{0,6},{2,4},{4,2},{6,0},{8,14},{10,12},{12,10},{14,8},{16,22},{18,... | collective-permute-start | bytes 98312 | tf_op jit(solution)/shard_map/ppermute | solution.py:323
  97.7 2.4 %collective-permute-start.23 = (f32[512,256]{1,0:T(8,128)}, f32[512,256]{1,0:T(8,128)S(1)}, u32[]{:S(2)}, u32[]{:S(2)}) collective-permute-start(f32[512,256]{1,0:T(8,128)} %collective-permute-done.12.r01), channel_id=1, source_target_pairs={{0,1},{1,0},{2,3},{3,2},{4,5},{5,4},{6,7},{7,6},{8,9},{9,8},{10,11... | collective-permute-start | bytes 1572872 | tf_op jit(solution)/shard_map/ppermute | solution.py:304
  100.2 3.5 %collective-permute-start.20 = (f32[512,256]{1,0:T(8,128)}, f32[512,256]{1,0:T(8,128)S(1)}, u32[]{:S(2)}, u32[]{:S(2)}) collective-permute-start(f32[512,256]{1,0:T(8,128)} %copy-done.7), channel_id=1, source_target_pairs={{0,2},{2,4},{4,6},{6,8},{8,10},{10,12},{12,14},{14,16},{16,18},{18... | collective-permute-start | bytes 1572872 | tf_op jit(solution)/shard_map/ppermute | solution.py:315
  103.8 2.8 %collective-permute-done.17 = f32[32,256]{1,0:T(8,128)S(1)} collective-permute-done((f32[32,256]{1,0:T(8,128)S(1)}, f32[32,256]{1,0:T(8,128)S(1)}, u32[]{:S(2)}, u32[]{:S(2)}) %collective-permute-start.17) | collective-permute-done | bytes 32800 | tf_op jit(solution)/shard_map/ppermute | solution.py:323
  106.5 4.1 %collective-permute-start.18 = (f32[32,256]{1,0:T(8,128)S(1)}, f32[32,256]{1,0:T(8,128)S(1)}, u32[]{:S(2)}, u32[]{:S(2)}) collective-permute-start(f32[32,256]{1,0:T(8,128)S(1)} %add.83), channel_id=1, source_target_pairs={{0,64},{32,96},{64,0},{96,32},{128,192},{160,224},{192,128},{224,1... | collective-permute-start | bytes 98312 | tf_op jit(solution)/shard_map/ppermute | solution.py:323
  112.0 5.0 %collective-permute-start.19 = (f32[32,256]{1,0:T(8,128)S(1)}, f32[32,256]{1,0:T(8,128)S(1)}, u32[]{:S(2)}, u32[]{:S(2)}) collective-permute-start(f32[32,256]{1,0:T(8,128)S(1)} %add.84), channel_id=1, source_target_pairs={{0,128},{32,160},{64,192},{96,224},{128,0},{160,32},{192,64},{224,... | collective-permute-start | bytes 98312 | tf_op jit(solution)/shard_map/ppermute | solution.py:323
  119.4 3.2 %collective-permute-start.26 = (f32[32,256]{1,0:T(8,128)S(1)}, f32[32,256]{1,0:T(8,128)S(1)}, u32[]{:S(2)}, u32[]{:S(2)}) collective-permute-start(f32[32,256]{1,0:T(8,128)S(1)} %add.85.refs_0_), channel_id=1, source_target_pairs={{0,6},{2,4},{4,2},{6,0},{8,14},{10,12},{12,10},{14,8},{16,22},{18,... | collective-permute-start | bytes 98312 | tf_op jit(solution)/shard_map/ppermute | solution.py:323
  122.7 7.4 %collective-permute-start.29 = (f32[512,256]{1,0:T(8,128)S(1)}, f32[512,256]{1,0:T(8,128)S(1)}, u32[]{:S(2)}, u32[]{:S(2)}) collective-permute-start(f32[512,256]{1,0:T(8,128)S(1)} %collective-permute-done.20.r00), channel_id=1, source_target_pairs={{0,1},{1,0},{2,3},{3,2},{4,5},{5,4},{6,7},{7,6},{8,9},{9,8},{10,11... | collective-permute-start | bytes 1572872 | tf_op jit(solution)/shard_map/ppermute | solution.py:304
  130.1 2.4 %collective-permute-start.27 = (f32[2,256,256]{2,1,0:T(8,128)}, f32[2,256,256]{2,1,0:T(8,128)S(1)}, u32[]{:S(2)}, u32[]{:S(2)}) collective-permute-start(f32[2,256,256]{2,1,0:T(8,128)} %copy-done.6), channel_id=1, source_target_pairs={{0,34},{2,36},{4,38},{6,40},{8,42},{10,44},{12,46},{14,48},{16,50}... | collective-permute-start | bytes 1572872 | tf_op jit(solution)/shard_map/ppermute | solution.py:315
  133.0 3.4 %collective-permute-start.32 = (f32[128,256]{1,0:T(8,128)S(1)}, f32[128,256]{1,0:T(8,128)S(1)}, u32[]{:S(2)}, u32[]{:S(2)}) collective-permute-start(f32[128,256]{1,0:T(8,128)S(1)} %bitcast.35), channel_id=1, source_target_pairs={{0,24},{2,26},{4,28},{6,30},{8,16},{10,18},{12,20},{14,22},{16,8},... | collective-permute-start | bytes 393224 | tf_op jit(solution)/shard_map/ppermute | solution.py:323
  136.5 4.5 %shard_map.81 = (f32[2,2,512,512]{3,2,1,0:T(8,128)}, f32[2,2,256,256]{3,2,1,0:T(8,128)S(1)}) custom-call(s32[1]{0:T(128)} %bitcast.scal, f32[2,512,512]{2,1,0:T(8,128)S(1)} %get-tuple-element.42.own0, f32[2,256,512]{2,1,0:T(8,128)S(1)} %collective-permute-done.16.b0, f32[512,256]{1,0:T(8,128)S(1)} %collective-permute-done.20.r00, ...), custom_call_target="tpu_custom_call" | custom-call | bytes 13631492 | tf_op jit(solution)/shard_map/pallas_call | solution.py:292
  140.9 6.2 %collective-permute-done.30.refs_1_ = f32[128,256]{1,0:T(8,128)S(1)} collective-permute-done((f32[128,256]{1,0:T(8,128)S(1)}, f32[128,256]{1,0:T(8,128)S(1)}, u32[]{:S(2)}, u32[]{:S(2)}) %collective-permute-start.30) | collective-permute-done | bytes 131104 | tf_op jit(solution)/shard_map/ppermute | solution.py:323
  147.2 3.2 %collective-permute-done.31.refs_2_ = f32[128,256]{1,0:T(8,128)S(1)} collective-permute-done((f32[128,256]{1,0:T(8,128)S(1)}, f32[128,256]{1,0:T(8,128)S(1)}, u32[]{:S(2)}, u32[]{:S(2)}) %collective-permute-start.31) | collective-permute-done | bytes 131104 | tf_op jit(solution)/shard_map/ppermute | solution.py:323
  (87 shorter events, 37.3 us)
Async XLA Ops:
  2.1 26.4 %collective-permute-start.1 = (f32[2,256,512]{2,1,0:T(8,128)S(1)}, f32[2,256,512]{2,1,0:T(8,128)S(1)}, u32[]{:S(2)}, u32[]{:S(2)}) collective-permute-start(f32[2,256,512]{2,1,0:T(8,128)S(1)} %dynamic-slice_bitcast_fusion.1), channel_id=1, source_target_pairs={{32,0},{34,2},{36,4},{38,6},{40,8},{42,10},{44,12},{46,14},{48,16}... | collective-permute-start | bytes 3145736 | tf_op jit(solution)/shard_map/ppermute | solution.py:315
  5.5 39.2 %collective-permute-start.2 = (f32[2,512,256]{2,1,0:T(8,128)S(1)}, f32[2,512,256]{2,1,0:T(8,128)S(1)}, u32[]{:S(2)}, u32[]{:S(2)}) collective-permute-start(f32[2,512,256]{2,1,0:T(8,128)S(1)} %dynamic-slice_bitcast_fusion), channel_id=1, source_target_pairs={{2,0},{4,2},{6,4},{8,6},{10,8},{12,10},{14,12},{16,14},{18,16},{20... | collective-permute-start | bytes 3145736 | tf_op jit(solution)/shard_map/ppermute | solution.py:315
  7.9 38.4 %collective-permute-start.3 = (f32[2,256,256]{2,1,0:T(8,128)S(1)}, f32[2,256,256]{2,1,0:T(8,128)S(1)}, u32[]{:S(2)}, u32[]{:S(2)}) collective-permute-start(f32[2,256,256]{2,1,0:T(8,128)S(1)} %dynamic-slice_bitcast_fusion.2), channel_id=1, source_target_pairs={{34,0},{36,2},{38,4},{40,6},{42,8},{44,10},{46,12},{48,14},{50,16}... | collective-permute-start | bytes 1572872 | tf_op jit(solution)/shard_map/ppermute | solution.py:315
  28.6 20.8 %collective-permute-start.4 = (f32[2,256,512]{2,1,0:T(8,128)S(1)}, f32[2,256,512]{2,1,0:T(8,128)S(1)}, u32[]{:S(2)}, u32[]{:S(2)}) collective-permute-start(f32[2,256,512]{2,1,0:T(8,128)S(1)} %collective-permute-done.1.b0), channel_id=1, source_target_pairs={{0,1},{1,0},{2,3},{3,2},{4,5},{5,4},{6,7},{7,6},{8,9},{9,8},{10,11... | collective-permute-start | bytes 3145736 | tf_op jit(solution)/shard_map/ppermute | solution.py:304
  63.9 26.5 %collective-permute-start.16 = (f32[2,256,512]{2,1,0:T(8,128)}, f32[2,256,512]{2,1,0:T(8,128)S(1)}, u32[]{:S(2)}, u32[]{:S(2)}) collective-permute-start(f32[2,256,512]{2,1,0:T(8,128)} %get-tuple-element.38), channel_id=1, source_target_pairs={{0,32},{2,34},{4,36},{6,38},{8,40},{10,42},{12,44},{14,46},{16,48}... | collective-permute-start | bytes 3145736 | tf_op jit(solution)/shard_map/ppermute | solution.py:315
  67.4 51.3 %collective-permute-start.21 = (f32[2,512,512]{2,1,0:T(8,128)S(1)}, f32[2,512,512]{2,1,0:T(8,128)}, u32[]{:S(2)}, u32[]{:S(2)}) collective-permute-start(f32[2,512,512]{2,1,0:T(8,128)S(1)} %get-tuple-element.42.own0), channel_id=1, source_target_pairs={{0,1},{1,0},{2,3},{3,2},{4,5},{5,4},{6,7},{7,6},{8,9},{9,8},{10,11... | collective-permute-start | bytes 6291464 | tf_op jit(solution)/shard_map/ppermute | solution.py:304
  68.4 25.4 %collective-permute-start.12 = (f32[512,256]{1,0:T(8,128)}, f32[512,256]{1,0:T(8,128)}, u32[]{:S(2)}, u32[]{:S(2)}) collective-permute-start(f32[512,256]{1,0:T(8,128)} %copy-done.8), channel_id=1, source_target_pairs={{0,2},{2,4},{4,6},{6,8},{8,10},{10,12},{12,14},{14,16},{16,18},{18... | collective-permute-start | bytes 1572872 | tf_op jit(solution)/shard_map/ppermute | solution.py:315
  75.1 13.2 %collective-permute-start.10 = (f32[128,256]{1,0:T(8,128)S(1)}, f32[128,256]{1,0:T(8,128)S(1)}, u32[]{:S(2)}, u32[]{:S(2)}) collective-permute-start(f32[128,256]{1,0:T(8,128)S(1)} %get-tuple-element.48), channel_id=1, source_target_pairs={{0,16},{2,18},{4,20},{6,22},{8,24},{10,26},{12,28},{14,30},{16,0},... | collective-permute-start | bytes 393224 | tf_op jit(solution)/shard_map/ppermute | solution.py:323
  78.0 13.6 %collective-permute-start.11 = (f32[128,256]{1,0:T(8,128)S(1)}, f32[128,256]{1,0:T(8,128)}, u32[]{:S(2)}, u32[]{:S(2)}) collective-permute-start(f32[128,256]{1,0:T(8,128)S(1)} %get-tuple-element.49), channel_id=1, source_target_pairs={{0,24},{2,26},{4,28},{6,30},{8,16},{10,18},{12,20},{14,22},{16,8},... | collective-permute-start | bytes 393224 | tf_op jit(solution)/shard_map/ppermute | solution.py:323
  90.3 28.4 %collective-permute-start.22 = (f32[2,256,512]{2,1,0:T(8,128)S(1)}, f32[2,256,512]{2,1,0:T(8,128)}, u32[]{:S(2)}, u32[]{:S(2)}) collective-permute-start(f32[2,256,512]{2,1,0:T(8,128)S(1)} %collective-permute-done.16.b0), channel_id=1, source_target_pairs={{0,1},{1,0},{2,3},{3,2},{4,5},{5,4},{6,7},{7,6},{8,9},{9,8},{10,11... | collective-permute-start | bytes 3145736 | tf_op jit(solution)/shard_map/ppermute | solution.py:304
  93.9 6.3 %collective-permute-start.14 = (f32[32,256]{1,0:T(8,128)S(1)}, f32[32,256]{1,0:T(8,128)S(1)}, u32[]{:S(2)}, u32[]{:S(2)}) collective-permute-start(f32[32,256]{1,0:T(8,128)S(1)} %get-tuple-element.51), channel_id=1, source_target_pairs={{0,4},{2,6},{4,0},{6,2},{8,12},{10,14},{12,8},{14,10},{16,20},{18,... | collective-permute-start | bytes 98312 | tf_op jit(solution)/shard_map/ppermute | solution.py:323
  94.0 6.2 %collective-permute-start.15 = (f32[32,256]{1,0:T(8,128)S(1)}, f32[32,256]{1,0:T(8,128)S(1)}, u32[]{:S(2)}, u32[]{:S(2)}) collective-permute-start(f32[32,256]{1,0:T(8,128)S(1)} %get-tuple-element.52), channel_id=1, source_target_pairs={{0,6},{2,4},{4,2},{6,0},{8,14},{10,12},{12,10},{14,8},{16,22},{18,... | collective-permute-start | bytes 98312 | tf_op jit(solution)/shard_map/ppermute | solution.py:323
  97.7 21.0 %collective-permute-start.23 = (f32[512,256]{1,0:T(8,128)}, f32[512,256]{1,0:T(8,128)S(1)}, u32[]{:S(2)}, u32[]{:S(2)}) collective-permute-start(f32[512,256]{1,0:T(8,128)} %collective-permute-done.12.r01), channel_id=1, source_target_pairs={{0,1},{1,0},{2,3},{3,2},{4,5},{5,4},{6,7},{7,6},{8,9},{9,8},{10,11... | collective-permute-start | bytes 1572872 | tf_op jit(solution)/shard_map/ppermute | solution.py:304
  100.2 18.5 %collective-permute-start.20 = (f32[512,256]{1,0:T(8,128)}, f32[512,256]{1,0:T(8,128)S(1)}, u32[]{:S(2)}, u32[]{:S(2)}) collective-permute-start(f32[512,256]{1,0:T(8,128)} %copy-done.7), channel_id=1, source_target_pairs={{0,2},{2,4},{4,6},{6,8},{8,10},{10,12},{12,14},{14,16},{16,18},{18... | collective-permute-start | bytes 1572872 | tf_op jit(solution)/shard_map/ppermute | solution.py:315
  106.5 5.4 %collective-permute-start.18 = (f32[32,256]{1,0:T(8,128)S(1)}, f32[32,256]{1,0:T(8,128)S(1)}, u32[]{:S(2)}, u32[]{:S(2)}) collective-permute-start(f32[32,256]{1,0:T(8,128)S(1)} %add.83), channel_id=1, source_target_pairs={{0,64},{32,96},{64,0},{96,32},{128,192},{160,224},{192,128},{224,1... | collective-permute-start | bytes 98312 | tf_op jit(solution)/shard_map/ppermute | solution.py:323
  112.0 6.7 %collective-permute-start.19 = (f32[32,256]{1,0:T(8,128)S(1)}, f32[32,256]{1,0:T(8,128)S(1)}, u32[]{:S(2)}, u32[]{:S(2)}) collective-permute-start(f32[32,256]{1,0:T(8,128)S(1)} %add.84), channel_id=1, source_target_pairs={{0,128},{32,160},{64,192},{96,224},{128,0},{160,32},{192,64},{224,... | collective-permute-start | bytes 98312 | tf_op jit(solution)/shard_map/ppermute | solution.py:323
  118.7 11.4 %collective-permute-start.24 = (f32[32,256]{1,0:T(8,128)S(1)}, f32[32,256]{1,0:T(8,128)S(1)}, u32[]{:S(2)}, u32[]{:S(2)}) collective-permute-start(f32[32,256]{1,0:T(8,128)S(1)} %add.85.refs_0_), channel_id=1, source_target_pairs={{0,2},{2,0},{4,6},{6,4},{8,10},{10,8},{12,14},{14,12},{16,18},{18,... | collective-permute-start | bytes 98312 | tf_op jit(solution)/shard_map/ppermute | solution.py:323
  118.8 11.3 %collective-permute-start.25 = (f32[32,256]{1,0:T(8,128)S(1)}, f32[32,256]{1,0:T(8,128)S(1)}, u32[]{:S(2)}, u32[]{:S(2)}) collective-permute-start(f32[32,256]{1,0:T(8,128)S(1)} %add.85.refs_0_), channel_id=1, source_target_pairs={{0,4},{2,6},{4,0},{6,2},{8,12},{10,14},{12,8},{14,10},{16,20},{18,... | collective-permute-start | bytes 98312 | tf_op jit(solution)/shard_map/ppermute | solution.py:323
  119.4 10.7 %collective-permute-start.26 = (f32[32,256]{1,0:T(8,128)S(1)}, f32[32,256]{1,0:T(8,128)S(1)}, u32[]{:S(2)}, u32[]{:S(2)}) collective-permute-start(f32[32,256]{1,0:T(8,128)S(1)} %add.85.refs_0_), channel_id=1, source_target_pairs={{0,6},{2,4},{4,2},{6,0},{8,14},{10,12},{12,10},{14,8},{16,22},{18,... | collective-permute-start | bytes 98312 | tf_op jit(solution)/shard_map/ppermute | solution.py:323
  122.7 13.8 %collective-permute-start.29 = (f32[512,256]{1,0:T(8,128)S(1)}, f32[512,256]{1,0:T(8,128)S(1)}, u32[]{:S(2)}, u32[]{:S(2)}) collective-permute-start(f32[512,256]{1,0:T(8,128)S(1)} %collective-permute-done.20.r00), channel_id=1, source_target_pairs={{0,1},{1,0},{2,3},{3,2},{4,5},{5,4},{6,7},{7,6},{8,9},{9,8},{10,11... | collective-permute-start | bytes 1572872 | tf_op jit(solution)/shard_map/ppermute | solution.py:304
  130.1 21.4 %collective-permute-start.27 = (f32[2,256,256]{2,1,0:T(8,128)}, f32[2,256,256]{2,1,0:T(8,128)S(1)}, u32[]{:S(2)}, u32[]{:S(2)}) collective-permute-start(f32[2,256,256]{2,1,0:T(8,128)} %copy-done.6), channel_id=1, source_target_pairs={{0,34},{2,36},{4,38},{6,40},{8,42},{10,44},{12,46},{14,48},{16,50}... | collective-permute-start | bytes 1572872 | tf_op jit(solution)/shard_map/ppermute | solution.py:315
  132.5 14.7 %collective-permute-start.30 = (f32[128,256]{1,0:T(8,128)S(1)}, f32[128,256]{1,0:T(8,128)S(1)}, u32[]{:S(2)}, u32[]{:S(2)}) collective-permute-start(f32[128,256]{1,0:T(8,128)S(1)} %bitcast.33), channel_id=1, source_target_pairs={{0,8},{2,10},{4,12},{6,14},{8,0},{10,2},{12,4},{14,6},{16,24},{18,... | collective-permute-start | bytes 393224 | tf_op jit(solution)/shard_map/ppermute | solution.py:323
  132.8 17.6 %collective-permute-start.31 = (f32[128,256]{1,0:T(8,128)S(1)}, f32[128,256]{1,0:T(8,128)S(1)}, u32[]{:S(2)}, u32[]{:S(2)}) collective-permute-start(f32[128,256]{1,0:T(8,128)S(1)} %bitcast.34), channel_id=1, source_target_pairs={{0,16},{2,18},{4,20},{6,22},{8,24},{10,26},{12,28},{14,30},{16,0},... | collective-permute-start | bytes 393224 | tf_op jit(solution)/shard_map/ppermute | solution.py:323
  133.0 17.4 %collective-permute-start.32 = (f32[128,256]{1,0:T(8,128)S(1)}, f32[128,256]{1,0:T(8,128)S(1)}, u32[]{:S(2)}, u32[]{:S(2)}) collective-permute-start(f32[128,256]{1,0:T(8,128)S(1)} %bitcast.35), channel_id=1, source_target_pairs={{0,24},{2,26},{4,28},{6,30},{8,16},{10,18},{12,20},{14,22},{16,8},... | collective-permute-start | bytes 393224 | tf_op jit(solution)/shard_map/ppermute | solution.py:323
  (21 other events, 111.7 us)

commit v4 on v3

--- a/solution.py
+++ b/solution.py
@@ -384,7 +384,7 @@
     v = scatter_sum(v.reshape(4, W // 2, W), x, 4)
     v = after(v, right1)
     v = scatter_sum(v.reshape(4, W // 8, W), y, 1)
-    v = after(v, below, right1)
+    v, own_sum, below, right1 = lax.optimization_barrier((v, own_sum, below, right1))
     others = [swap(t) for t in (own_sum, below, right1)]
     right0 = shift(after(right0, v), 0, 1)
     for bit in (1, 2, 4):

time: 156 us -> 153 us (0.981)
  starting transfers between devices: 60.1 us -> 58.5 us
    ppermute x15, waiting for transfers between devices: 25.8 us -> 31.4 us  [exchange(): lax.ppermute(x, axis, [(i, i ^ bits) for i in range(lax.axis_size(axis))])]
    ppermute x12, starting transfers between devices: 17.7 us -> 14.2 us  [swap(): return lax.ppermute(x, 'scan', [(0, 1), (1, 0)])]
    ppermute x7, starting transfers between devices: 17.6 us -> 20.9 us  [shift(): return lax.ppermute(x, ('tx', 'ty'), route)]
    ppermute x12, waiting for transfers between devices: 8.53 us -> 5.43 us  [swap(): return lax.ppermute(x, 'scan', [(0, 1), (1, 0)])]
    ppermute x7, waiting for transfers between devices: 30.9 us -> 28.7 us  [shift(): return lax.ppermute(x, ('tx', 'ty'), route)]
    unnamed x22 -> x20, local copies, waits for them, and re-layouts: 5.11 us -> 4.33 us
  transfers between devices with their start and end apart: 34 -> 34, of which waited for: 14 -> 13; matrix products, arithmetic and copies ran while one was open for 3% -> 3% of each run, Pallas kernels for 5% -> 6%
where the time goes in v4:
time: 153 us
  waiting for transfers between devices  65.5 us (43%)
  starting transfers between devices  58.5 us (38%)
  Pallas kernels  17.6 us (12%)
  local copies, waits for them, and re-layouts  7.84 us (5%)
  other arithmetic  2.51 us (2%)
    ppermute x15, waiting for transfers between devices, exchange(): lax.ppermute(x, axis, [(i, i ^ bits) for i in range(lax.axis_size(axis))])  31.4 us
    ppermute x7, waiting for transfers between devices, shift(): return lax.ppermute(x, ('tx', 'ty'), route)  28.7 us
    ppermute x15, starting transfers between devices, exchange(): lax.ppermute(x, axis, [(i, i ^ bits) for i in range(lax.axis_size(axis))])  23.4 us
    ppermute x7, starting transfers between devices, shift(): return lax.ppermute(x, ('tx', 'ty'), route)  20.9 us
    pallas_call x7, Pallas kernels, call(): pl.pallas_call(kernel, out_shape=[jax.ShapeDtypeStruct(o, F32) for o in o...  16.6 us
    ppermute x12, starting transfers between devices, swap(): return lax.ppermute(x, 'scan', [(0, 1), (1, 0)])  14.2 us
    ppermute x12, waiting for transfers between devices, swap(): return lax.ppermute(x, 'scan', [(0, 1), (1, 0)])  5.43 us
    unnamed x20, local copies, waits for them, and re-layouts  4.33 us
  transfers between devices with their start and end apart: 34, of which 13 were waited for; matrix products, arithmetic and copies ran while one was open for 3% of the time, Pallas kernels for 6%

profile of v4, /device:TPU:57, one launch (start us, length us, event | category | flops | bytes accessed | tf_op | source)
XLA Modules:
  0.0 153.0 jit_solution(14343558324261581083)
XLA Ops:
  5.5 2.4 %collective-permute-start.2 = (f32[2,512,256]{2,1,0:T(8,128)S(1)}, f32[2,512,256]{2,1,0:T(8,128)S(1)}, u32[]{:S(2)}, u32[]{:S(2)}) collective-permute-start(f32[2,512,256]{2,1,0:T(8,128)S(1)} %dynamic-slice_bitcast_fusion), channel_id=1, source_target_pairs={{2,0},{4,2},{6,4},{8,6},{10,8},{12,10},{14,12},{16,14},{18,16},{20... | collective-permute-start | bytes 3145736 | tf_op jit(solution)/shard_map/ppermute | solution.py:315
  13.7 14.9 %collective-permute-done.1.b0 = f32[2,256,512]{2,1,0:T(8,128)S(1)} collective-permute-done((f32[2,256,512]{2,1,0:T(8,128)S(1)}, f32[2,256,512]{2,1,0:T(8,128)S(1)}, u32[]{:S(2)}, u32[]{:S(2)}) %collective-permute-start.1) | collective-permute-done | bytes 1048608 | tf_op jit(solution)/shard_map/ppermute | solution.py:315
  28.6 2.3 %collective-permute-start.4 = (f32[2,256,512]{2,1,0:T(8,128)S(1)}, f32[2,256,512]{2,1,0:T(8,128)S(1)}, u32[]{:S(2)}, u32[]{:S(2)}) collective-permute-start(f32[2,256,512]{2,1,0:T(8,128)S(1)} %collective-permute-done.1.b0), channel_id=1, source_target_pairs={{0,1},{1,0},{2,3},{3,2},{4,5},{5,4},{6,7},{7,6},{8,9},{9,8},{10,11... | collective-permute-start | bytes 3145736 | tf_op jit(solution)/shard_map/ppermute | solution.py:304
  30.8 13.8 %collective-permute-done.2.r0 = f32[2,512,256]{2,1,0:T(8,128)S(1)} collective-permute-done((f32[2,512,256]{2,1,0:T(8,128)S(1)}, f32[2,512,256]{2,1,0:T(8,128)S(1)}, u32[]{:S(2)}, u32[]{:S(2)}) %collective-permute-start.2) | collective-permute-done | bytes 1048608 | tf_op jit(solution)/shard_map/ppermute | solution.py:315
  46.4 3.0 %collective-permute-done.6.d1 = f32[2,256,256]{2,1,0:T(8,128)S(1)} collective-permute-done((f32[2,256,256]{2,1,0:T(8,128)S(1)}, f32[2,256,256]{2,1,0:T(8,128)S(1)}, u32[]{:S(2)}, u32[]{:S(2)}) %collective-permute-start.6) | collective-permute-done | bytes 524320 | tf_op jit(solution)/shard_map/ppermute | solution.py:304
  49.4 7.4 %shard_map.78 = (f32[2,256,256]{2,1,0:T(8,128)S(1)}, f32[2,256,256]{2,1,0:T(8,128)S(1)}, f32[2,256,256]{2,1,0:T(8,128)S(1)}, f32[2,256,256]{2,1,0:T(8,128)}) custom-call(s32[3]{0:T(128)S(1)} %pad_add_fusion.1.scal, f32[2,2,256,256]{3,2,1,0:T(8,128)S(1)} %get-tuple-element.28.own, f32[2,256,512]{2,1,0:T(8,128)S(1)} %collective-permute-done.1.b0, ...), custom_call_target="tpu_custom_call" | custom-call | flops 3221225472 | bytes 11796492 | tf_op jit(solution)/shard_map/pallas_call | solution.py:292
  58.8 2.6 %shard_map.79 = (f32[2,512,512]{2,1,0:T(8,128)S(1)}, f32[2,256,512]{2,1,0:T(8,128)}, f32[512,256]{1,0:T(8,128)S(1)}, f32[512,256]{1,0:T(8,128)}, f32[2,256,256]{2,1,0:T(8,128)S(1)}) custom-call(s32[4]{0:T(128)S(1)} %pad_add_fusion.scal, f32[2,256,256]{2,1,0:T(8,128)S(1)} %get-tuple-element.34.mine, f32[2,256,256]{2,1,0:T(8,128)S(1)} %collective-permute-done.7.other), custom_call_target="tpu_custom_call" | custom-call | bytes 5767184 | tf_op jit(solution)/shard_map/pallas_call | solution.py:292
  63.0 3.5 %collective-permute-start.16 = (f32[2,256,512]{2,1,0:T(8,128)}, f32[2,256,512]{2,1,0:T(8,128)S(1)}, u32[]{:S(2)}, u32[]{:S(2)}) collective-permute-start(f32[2,256,512]{2,1,0:T(8,128)} %get-tuple-element.42), channel_id=1, source_target_pairs={{0,32},{2,34},{4,36},{6,38},{8,40},{10,42},{12,44},{14,46},{16,48}... | collective-permute-start | bytes 3145736 | tf_op jit(solution)/shard_map/ppermute | solution.py:315
  71.3 2.7 %collective-permute-start.10 = (f32[128,256]{1,0:T(8,128)}, f32[128,256]{1,0:T(8,128)S(1)}, u32[]{:S(2)}, u32[]{:S(2)}) collective-permute-start(f32[128,256]{1,0:T(8,128)} %get-tuple-element.54), channel_id=1, source_target_pairs={{0,16},{2,18},{4,20},{6,22},{8,24},{10,26},{12,28},{14,30},{16,0},... | collective-permute-start | bytes 393224 | tf_op jit(solution)/shard_map/ppermute | solution.py:323
  74.8 11.1 %collective-permute-done.10 = f32[128,256]{1,0:T(8,128)S(1)} collective-permute-done((f32[128,256]{1,0:T(8,128)}, f32[128,256]{1,0:T(8,128)S(1)}, u32[]{:S(2)}, u32[]{:S(2)}) %collective-permute-start.10) | collective-permute-done | bytes 131104 | tf_op jit(solution)/shard_map/ppermute | solution.py:323
  87.2 3.7 %collective-permute-start.15 = (f32[32,256]{1,0:T(8,128)S(1)}, f32[32,256]{1,0:T(8,128)S(1)}, u32[]{:S(2)}, u32[]{:S(2)}) collective-permute-start(f32[32,256]{1,0:T(8,128)S(1)} %get-tuple-element.58), channel_id=1, source_target_pairs={{0,6},{2,4},{4,2},{6,0},{8,14},{10,12},{12,10},{14,8},{16,22},{18,... | collective-permute-start | bytes 98312 | tf_op jit(solution)/shard_map/ppermute | solution.py:323
  92.3 3.5 %collective-permute-start.21 = (f32[2,512,512]{2,1,0:T(8,128)S(1)}, f32[2,512,512]{2,1,0:T(8,128)S(1)}, u32[]{:S(2)}, u32[]{:S(2)}) collective-permute-start(f32[2,512,512]{2,1,0:T(8,128)S(1)} %get-tuple-element.46.own0), channel_id=1, source_target_pairs={{0,1},{1,0},{2,3},{3,2},{4,5},{5,4},{6,7},{7,6},{8,9},{9,8},{10,11... | collective-permute-start | bytes 6291464 | tf_op jit(solution)/shard_map/ppermute | solution.py:304
  95.9 5.4 %collective-permute-start.20 = (f32[512,256]{1,0:T(8,128)}, f32[512,256]{1,0:T(8,128)S(1)}, u32[]{:S(2)}, u32[]{:S(2)}) collective-permute-start(f32[512,256]{1,0:T(8,128)} %copy-done.7), channel_id=1, source_target_pairs={{0,2},{2,4},{4,6},{6,8},{8,10},{10,12},{12,14},{14,16},{16,18},{18... | collective-permute-start | bytes 1572872 | tf_op jit(solution)/shard_map/ppermute | solution.py:315
  102.1 3.1 %collective-permute-done.17 = f32[32,256]{1,0:T(8,128)S(1)} collective-permute-done((f32[32,256]{1,0:T(8,128)S(1)}, f32[32,256]{1,0:T(8,128)S(1)}, u32[]{:S(2)}, u32[]{:S(2)}) %collective-permute-start.17) | collective-permute-done | bytes 32800 | tf_op jit(solution)/shard_map/ppermute | solution.py:323
  105.2 4.2 %collective-permute-start.18 = (f32[32,256]{1,0:T(8,128)S(1)}, f32[32,256]{1,0:T(8,128)S(1)}, u32[]{:S(2)}, u32[]{:S(2)}) collective-permute-start(f32[32,256]{1,0:T(8,128)S(1)} %add.83), channel_id=1, source_target_pairs={{0,64},{32,96},{64,0},{96,32},{128,192},{160,224},{192,128},{224,1... | collective-permute-start | bytes 98312 | tf_op jit(solution)/shard_map/ppermute | solution.py:323
  110.8 3.9 %collective-permute-start.19 = (f32[32,256]{1,0:T(8,128)S(1)}, f32[32,256]{1,0:T(8,128)S(1)}, u32[]{:S(2)}, u32[]{:S(2)}) collective-permute-start(f32[32,256]{1,0:T(8,128)S(1)} %add.84), channel_id=1, source_target_pairs={{0,128},{32,160},{64,192},{96,224},{128,0},{160,32},{192,64},{224,... | collective-permute-start | bytes 98312 | tf_op jit(solution)/shard_map/ppermute | solution.py:323
  114.7 2.8 %collective-permute-done.19 = f32[32,256]{1,0:T(8,128)S(1)} collective-permute-done((f32[32,256]{1,0:T(8,128)S(1)}, f32[32,256]{1,0:T(8,128)S(1)}, u32[]{:S(2)}, u32[]{:S(2)}) %collective-permute-start.19) | collective-permute-done | bytes 32800 | tf_op jit(solution)/shard_map/ppermute | solution.py:323
  117.7 3.7 %collective-permute-start.26 = (f32[32,256]{1,0:T(8,128)S(1)}, f32[32,256]{1,0:T(8,128)S(1)}, u32[]{:S(2)}, u32[]{:S(2)}) collective-permute-start(f32[32,256]{1,0:T(8,128)S(1)} %add.85.refs_0_), channel_id=1, source_target_pairs={{0,6},{2,4},{4,2},{6,0},{8,14},{10,12},{12,10},{14,8},{16,22},{18,... | collective-permute-start | bytes 98312 | tf_op jit(solution)/shard_map/ppermute | solution.py:323
  121.5 4.0 %collective-permute-start.29 = (f32[512,256]{1,0:T(8,128)S(1)}, f32[512,256]{1,0:T(8,128)S(1)}, u32[]{:S(2)}, u32[]{:S(2)}) collective-permute-start(f32[512,256]{1,0:T(8,128)S(1)} %collective-permute-done.20.r00), channel_id=1, source_target_pairs={{0,1},{1,0},{2,3},{3,2},{4,5},{5,4},{6,7},{7,6},{8,9},{9,8},{10,11... | collective-permute-start | bytes 1572872 | tf_op jit(solution)/shard_map/ppermute | solution.py:304
  125.5 3.6 %collective-permute-start.27 = (f32[2,256,256]{2,1,0:T(8,128)}, f32[2,256,256]{2,1,0:T(8,128)S(1)}, u32[]{:S(2)}, u32[]{:S(2)}) collective-permute-start(f32[2,256,256]{2,1,0:T(8,128)} %copy-done.6), channel_id=1, source_target_pairs={{0,34},{2,36},{4,38},{6,40},{8,42},{10,44},{12,46},{14,48},{16,50}... | collective-permute-start | bytes 1572872 | tf_op jit(solution)/shard_map/ppermute | solution.py:315
  130.8 2.3 %collective-permute-start.32 = (f32[128,256]{1,0:T(8,128)S(1)}, f32[128,256]{1,0:T(8,128)S(1)}, u32[]{:S(2)}, u32[]{:S(2)}) collective-permute-start(f32[128,256]{1,0:T(8,128)S(1)} %bitcast.35), channel_id=1, source_target_pairs={{0,24},{2,26},{4,28},{6,30},{8,16},{10,18},{12,20},{14,22},{16,8},... | collective-permute-start | bytes 393224 | tf_op jit(solution)/shard_map/ppermute | solution.py:323
  133.1 3.6 %shard_map.81 = (f32[2,2,512,512]{3,2,1,0:T(8,128)}, f32[2,2,256,256]{3,2,1,0:T(8,128)S(1)}) custom-call(s32[1]{0:T(128)} %bitcast.scal, f32[2,512,512]{2,1,0:T(8,128)S(1)} %get-tuple-element.46.own0, f32[2,256,512]{2,1,0:T(8,128)S(1)} %collective-permute-done.16.b0, f32[512,256]{1,0:T(8,128)S(1)} %collective-permute-done.20.r00, ...), custom_call_target="tpu_custom_call" | custom-call | bytes 13631492 | tf_op jit(solution)/shard_map/pallas_call | solution.py:292
  136.7 7.1 %collective-permute-done.30.refs_1_ = f32[128,256]{1,0:T(8,128)S(1)} collective-permute-done((f32[128,256]{1,0:T(8,128)S(1)}, f32[128,256]{1,0:T(8,128)S(1)}, u32[]{:S(2)}, u32[]{:S(2)}) %collective-permute-start.30) | collective-permute-done | bytes 131104 | tf_op jit(solution)/shard_map/ppermute | solution.py:323
  143.7 4.7 %collective-permute-done.31.refs_2_ = f32[128,256]{1,0:T(8,128)S(1)} collective-permute-done((f32[128,256]{1,0:T(8,128)S(1)}, f32[128,256]{1,0:T(8,128)S(1)}, u32[]{:S(2)}, u32[]{:S(2)}) %collective-permute-start.31) | collective-permute-done | bytes 131104 | tf_op jit(solution)/shard_map/ppermute | solution.py:323
  (85 shorter events, 32.8 us)
Async XLA Ops:
  2.1 26.4 %collective-permute-start.1 = (f32[2,256,512]{2,1,0:T(8,128)S(1)}, f32[2,256,512]{2,1,0:T(8,128)S(1)}, u32[]{:S(2)}, u32[]{:S(2)}) collective-permute-start(f32[2,256,512]{2,1,0:T(8,128)S(1)} %dynamic-slice_bitcast_fusion.1), channel_id=1, source_target_pairs={{32,0},{34,2},{36,4},{38,6},{40,8},{42,10},{44,12},{46,14},{48,16}... | collective-permute-start | bytes 3145736 | tf_op jit(solution)/shard_map/ppermute | solution.py:315
  5.5 39.2 %collective-permute-start.2 = (f32[2,512,256]{2,1,0:T(8,128)S(1)}, f32[2,512,256]{2,1,0:T(8,128)S(1)}, u32[]{:S(2)}, u32[]{:S(2)}) collective-permute-start(f32[2,512,256]{2,1,0:T(8,128)S(1)} %dynamic-slice_bitcast_fusion), channel_id=1, source_target_pairs={{2,0},{4,2},{6,4},{8,6},{10,8},{12,10},{14,12},{16,14},{18,16},{20... | collective-permute-start | bytes 3145736 | tf_op jit(solution)/shard_map/ppermute | solution.py:315
  7.9 38.4 %collective-permute-start.3 = (f32[2,256,256]{2,1,0:T(8,128)S(1)}, f32[2,256,256]{2,1,0:T(8,128)S(1)}, u32[]{:S(2)}, u32[]{:S(2)}) collective-permute-start(f32[2,256,256]{2,1,0:T(8,128)S(1)} %dynamic-slice_bitcast_fusion.2), channel_id=1, source_target_pairs={{34,0},{36,2},{38,4},{40,6},{42,8},{44,10},{46,12},{48,14},{50,16}... | collective-permute-start | bytes 1572872 | tf_op jit(solution)/shard_map/ppermute | solution.py:315
  28.6 20.8 %collective-permute-start.4 = (f32[2,256,512]{2,1,0:T(8,128)S(1)}, f32[2,256,512]{2,1,0:T(8,128)S(1)}, u32[]{:S(2)}, u32[]{:S(2)}) collective-permute-start(f32[2,256,512]{2,1,0:T(8,128)S(1)} %collective-permute-done.1.b0), channel_id=1, source_target_pairs={{0,1},{1,0},{2,3},{3,2},{4,5},{5,4},{6,7},{7,6},{8,9},{9,8},{10,11... | collective-permute-start | bytes 3145736 | tf_op jit(solution)/shard_map/ppermute | solution.py:304
  57.2 11.3 %collective-permute-start.8 = (f32[2,256,256]{2,1,0:T(8,128)}, f32[2,256,256]{2,1,0:T(8,128)}, u32[]{:S(2)}, u32[]{:S(2)}) collective-permute-start(f32[2,256,256]{2,1,0:T(8,128)} %get-tuple-element.38), channel_id=1, source_target_pairs={{0,1},{1,0},{2,3},{3,2},{4,5},{5,4},{6,7},{7,6},{8,9},{9,8},{10,11... | collective-permute-start | bytes 1572872 | tf_op jit(solution)/shard_map/ppermute | solution.py:304
  63.0 29.3 %collective-permute-start.16 = (f32[2,256,512]{2,1,0:T(8,128)}, f32[2,256,512]{2,1,0:T(8,128)S(1)}, u32[]{:S(2)}, u32[]{:S(2)}) collective-permute-start(f32[2,256,512]{2,1,0:T(8,128)} %get-tuple-element.42), channel_id=1, source_target_pairs={{0,32},{2,34},{4,36},{6,38},{8,40},{10,42},{12,44},{14,46},{16,48}... | collective-permute-start | bytes 3145736 | tf_op jit(solution)/shard_map/ppermute | solution.py:315
  66.6 20.4 %collective-permute-start.12 = (f32[512,256]{1,0:T(8,128)}, f32[512,256]{1,0:T(8,128)}, u32[]{:S(2)}, u32[]{:S(2)}) collective-permute-start(f32[512,256]{1,0:T(8,128)} %get-tuple-element.39), channel_id=1, source_target_pairs={{0,2},{2,4},{4,6},{6,8},{8,10},{10,12},{12,14},{14,16},{16,18},{18... | collective-permute-start | bytes 1572872 | tf_op jit(solution)/shard_map/ppermute | solution.py:315
  71.3 14.6 %collective-permute-start.10 = (f32[128,256]{1,0:T(8,128)}, f32[128,256]{1,0:T(8,128)S(1)}, u32[]{:S(2)}, u32[]{:S(2)}) collective-permute-start(f32[128,256]{1,0:T(8,128)} %get-tuple-element.54), channel_id=1, source_target_pairs={{0,16},{2,18},{4,20},{6,22},{8,24},{10,26},{12,28},{14,30},{16,0},... | collective-permute-start | bytes 393224 | tf_op jit(solution)/shard_map/ppermute | solution.py:323
  74.0 11.9 %collective-permute-start.11 = (f32[128,256]{1,0:T(8,128)S(1)}, f32[128,256]{1,0:T(8,128)}, u32[]{:S(2)}, u32[]{:S(2)}) collective-permute-start(f32[128,256]{1,0:T(8,128)S(1)} %get-tuple-element.55), channel_id=1, source_target_pairs={{0,24},{2,26},{4,28},{6,30},{8,16},{10,18},{12,20},{14,22},{16,8},... | collective-permute-start | bytes 393224 | tf_op jit(solution)/shard_map/ppermute | solution.py:323
  74.8 11.1 %collective-permute-start.9 = (f32[128,256]{1,0:T(8,128)S(1)}, f32[128,256]{1,0:T(8,128)}, u32[]{:S(2)}, u32[]{:S(2)}) collective-permute-start(f32[128,256]{1,0:T(8,128)S(1)} %get-tuple-element.56), channel_id=1, source_target_pairs={{0,8},{2,10},{4,12},{6,14},{8,0},{10,2},{12,4},{14,6},{16,24},{18,... | collective-permute-start | bytes 393224 | tf_op jit(solution)/shard_map/ppermute | solution.py:323
  92.3 25.2 %collective-permute-start.21 = (f32[2,512,512]{2,1,0:T(8,128)S(1)}, f32[2,512,512]{2,1,0:T(8,128)S(1)}, u32[]{:S(2)}, u32[]{:S(2)}) collective-permute-start(f32[2,512,512]{2,1,0:T(8,128)S(1)} %get-tuple-element.46.own0), channel_id=1, source_target_pairs={{0,1},{1,0},{2,3},{3,2},{4,5},{5,4},{6,7},{7,6},{8,9},{9,8},{10,11... | collective-permute-start | bytes 6291464 | tf_op jit(solution)/shard_map/ppermute | solution.py:304
  95.8 21.7 %collective-permute-start.22 = (f32[2,256,512]{2,1,0:T(8,128)S(1)}, f32[2,256,512]{2,1,0:T(8,128)S(1)}, u32[]{:S(2)}, u32[]{:S(2)}) collective-permute-start(f32[2,256,512]{2,1,0:T(8,128)S(1)} %collective-permute-done.16.b0), channel_id=1, source_target_pairs={{0,1},{1,0},{2,3},{3,2},{4,5},{5,4},{6,7},{7,6},{8,9},{9,8},{10,11... | collective-permute-start | bytes 3145736 | tf_op jit(solution)/shard_map/ppermute | solution.py:304
  95.9 21.6 %collective-permute-start.20 = (f32[512,256]{1,0:T(8,128)}, f32[512,256]{1,0:T(8,128)S(1)}, u32[]{:S(2)}, u32[]{:S(2)}) collective-permute-start(f32[512,256]{1,0:T(8,128)} %copy-done.7), channel_id=1, source_target_pairs={{0,2},{2,4},{4,6},{6,8},{8,10},{10,12},{12,14},{14,16},{16,18},{18... | collective-permute-start | bytes 1572872 | tf_op jit(solution)/shard_map/ppermute | solution.py:315
  101.3 16.1 %collective-permute-start.23 = (f32[512,256]{1,0:T(8,128)}, f32[512,256]{1,0:T(8,128)S(1)}, u32[]{:S(2)}, u32[]{:S(2)}) collective-permute-start(f32[512,256]{1,0:T(8,128)} %collective-permute-done.12.r01), channel_id=1, source_target_pairs={{0,1},{1,0},{2,3},{3,2},{4,5},{5,4},{6,7},{7,6},{8,9},{9,8},{10,11... | collective-permute-start | bytes 1572872 | tf_op jit(solution)/shard_map/ppermute | solution.py:304
  105.2 5.6 %collective-permute-start.18 = (f32[32,256]{1,0:T(8,128)S(1)}, f32[32,256]{1,0:T(8,128)S(1)}, u32[]{:S(2)}, u32[]{:S(2)}) collective-permute-start(f32[32,256]{1,0:T(8,128)S(1)} %add.83), channel_id=1, source_target_pairs={{0,64},{32,96},{64,0},{96,32},{128,192},{160,224},{192,128},{224,1... | collective-permute-start | bytes 98312 | tf_op jit(solution)/shard_map/ppermute | solution.py:323
  110.8 6.7 %collective-permute-start.19 = (f32[32,256]{1,0:T(8,128)S(1)}, f32[32,256]{1,0:T(8,128)S(1)}, u32[]{:S(2)}, u32[]{:S(2)}) collective-permute-start(f32[32,256]{1,0:T(8,128)S(1)} %add.84), channel_id=1, source_target_pairs={{0,128},{32,160},{64,192},{96,224},{128,0},{160,32},{192,64},{224,... | collective-permute-start | bytes 98312 | tf_op jit(solution)/shard_map/ppermute | solution.py:323
  117.5 7.9 %collective-permute-start.24 = (f32[32,256]{1,0:T(8,128)S(1)}, f32[32,256]{1,0:T(8,128)S(1)}, u32[]{:S(2)}, u32[]{:S(2)}) collective-permute-start(f32[32,256]{1,0:T(8,128)S(1)} %add.85.refs_0_), channel_id=1, source_target_pairs={{0,2},{2,0},{4,6},{6,4},{8,10},{10,8},{12,14},{14,12},{16,18},{18,... | collective-permute-start | bytes 98312 | tf_op jit(solution)/shard_map/ppermute | solution.py:323
  117.6 7.9 %collective-permute-start.25 = (f32[32,256]{1,0:T(8,128)S(1)}, f32[32,256]{1,0:T(8,128)S(1)}, u32[]{:S(2)}, u32[]{:S(2)}) collective-permute-start(f32[32,256]{1,0:T(8,128)S(1)} %add.85.refs_0_), channel_id=1, source_target_pairs={{0,4},{2,6},{4,0},{6,2},{8,12},{10,14},{12,8},{14,10},{16,20},{18,... | collective-permute-start | bytes 98312 | tf_op jit(solution)/shard_map/ppermute | solution.py:323
  117.7 7.8 %collective-permute-start.26 = (f32[32,256]{1,0:T(8,128)S(1)}, f32[32,256]{1,0:T(8,128)S(1)}, u32[]{:S(2)}, u32[]{:S(2)}) collective-permute-start(f32[32,256]{1,0:T(8,128)S(1)} %add.85.refs_0_), channel_id=1, source_target_pairs={{0,6},{2,4},{4,2},{6,0},{8,14},{10,12},{12,10},{14,8},{16,22},{18,... | collective-permute-start | bytes 98312 | tf_op jit(solution)/shard_map/ppermute | solution.py:323
  121.5 11.6 %collective-permute-start.29 = (f32[512,256]{1,0:T(8,128)S(1)}, f32[512,256]{1,0:T(8,128)S(1)}, u32[]{:S(2)}, u32[]{:S(2)}) collective-permute-start(f32[512,256]{1,0:T(8,128)S(1)} %collective-permute-done.20.r00), channel_id=1, source_target_pairs={{0,1},{1,0},{2,3},{3,2},{4,5},{5,4},{6,7},{7,6},{8,9},{9,8},{10,11... | collective-permute-start | bytes 1572872 | tf_op jit(solution)/shard_map/ppermute | solution.py:304
  125.5 23.9 %collective-permute-start.27 = (f32[2,256,256]{2,1,0:T(8,128)}, f32[2,256,256]{2,1,0:T(8,128)S(1)}, u32[]{:S(2)}, u32[]{:S(2)}) collective-permute-start(f32[2,256,256]{2,1,0:T(8,128)} %copy-done.6), channel_id=1, source_target_pairs={{0,34},{2,36},{4,38},{6,40},{8,42},{10,44},{12,46},{14,48},{16,50}... | collective-permute-start | bytes 1572872 | tf_op jit(solution)/shard_map/ppermute | solution.py:315
  129.1 14.6 %collective-permute-start.30 = (f32[128,256]{1,0:T(8,128)S(1)}, f32[128,256]{1,0:T(8,128)S(1)}, u32[]{:S(2)}, u32[]{:S(2)}) collective-permute-start(f32[128,256]{1,0:T(8,128)S(1)} %bitcast.33), channel_id=1, source_target_pairs={{0,8},{2,10},{4,12},{6,14},{8,0},{10,2},{12,4},{14,6},{16,24},{18,... | collective-permute-start | bytes 393224 | tf_op jit(solution)/shard_map/ppermute | solution.py:323
  130.5 17.9 %collective-permute-start.31 = (f32[128,256]{1,0:T(8,128)S(1)}, f32[128,256]{1,0:T(8,128)S(1)}, u32[]{:S(2)}, u32[]{:S(2)}) collective-permute-start(f32[128,256]{1,0:T(8,128)S(1)} %bitcast.34), channel_id=1, source_target_pairs={{0,16},{2,18},{4,20},{6,22},{8,24},{10,26},{12,28},{14,30},{16,0},... | collective-permute-start | bytes 393224 | tf_op jit(solution)/shard_map/ppermute | solution.py:323
  130.8 17.6 %collective-permute-start.32 = (f32[128,256]{1,0:T(8,128)S(1)}, f32[128,256]{1,0:T(8,128)S(1)}, u32[]{:S(2)}, u32[]{:S(2)}) collective-permute-start(f32[128,256]{1,0:T(8,128)S(1)} %bitcast.35), channel_id=1, source_target_pairs={{0,24},{2,26},{4,28},{6,30},{8,16},{10,18},{12,20},{14,22},{16,8},... | collective-permute-start | bytes 393224 | tf_op jit(solution)/shard_map/ppermute | solution.py:323
  (20 other events, 104.8 us)
